TPU v7x, 32 devices: a whole 2x2x4 slice. The times are simulated.
32 devices in a mesh: pipe: 4 (over z), dp: 8 (over y, x, core).
Axes of the slice: x: 2, y: 2, z: 4, core: 2. Of those that a mesh axis runs over, the one named last changes fastest.
Arguments:
- acts_in: bfloat16 [2, 512, 4096], P(None, 'dp'), may hold values from -40 to 40
- cotangent: bfloat16 [2, 512, 4096], P(None, 'dp'), may hold values from -6 to 6
- norm_gains: float32 [4, 4096], P('pipe'), may hold values from 0.1 to 1.9
- weights: bfloat16 [4, 256, 128, 128], P('pipe', 'dp'), may hold values from -0.1875 to 0.1875
- tile_columns: int32 [4, 256], P('pipe'), may hold values from 0 to 31, as said below
- lengths: int32 [2, 8], P(None, 'dp'), may hold values from 16 to 64
Outputs:
- section_out: bfloat16 [4, 2, 512, 4096], P('pipe', None, 'dp')
- input_grad: bfloat16 [4, 2, 512, 4096], P('pipe', None, 'dp')
- weight_grad: float32 [4, 256, 128, 128], P('pipe', 'dp')
Inputs may be any that keep to these rules, and one draw needn't show every extreme that they name: `tile_columns`: the 8 entries of one block row of a section (positions r * 8 to r * 8 + 7) are distinct.
All inputs are finite; a program needn't handle non-finite values.
Results may differ from a plain program's by a relative error of at most 0.0081.
Values may be sent and summed in bfloat16 or wider, within the bound.
A program may use at most 384 MiB of HBM per device.

v0:
```python
import functools

import jax
import jax.numpy as jnp
from jax import lax
from jax.experimental import pallas as pl
from jax.experimental.pallas import tpu as pltpu
from jax.sharding import PartitionSpec as P

KEEP = 8
EPSILON = 1e-05
ROWS_PER_STEP = 4
VMEM_BYTES = 48 * 1024 * 1024

F32 = jnp.float32
BF16 = jnp.bfloat16


def sigmoid(v):
    return 1.0 / (1.0 + jnp.exp(-v))


def columns(block, tile):
    return pl.ds(block * tile, tile)


def forward_kernel(state, cols, acts, received, gain, tiles, *refs):
    y_ref, out_ref, x_ref, pre_ref, hid_ref = refs[-5:]
    blocks, _, tile = pre_ref.shape[1:]
    step = pl.program_id(0)
    live = state[0] > 0
    first = state[2] > 0

    @pl.when(jnp.logical_and(live, step == 0))
    def _():
        @pl.when(first)
        def _():
            x_ref[0] = acts[0]

        @pl.when(jnp.logical_not(first))
        def _():
            x_ref[0] = received[...]

        total = jnp.zeros(pre_ref.shape[2:], F32)
        for r in range(blocks):
            v = x_ref[0, :, columns(r, tile)].astype(F32)
            total = total + v * v
        mean = jnp.sum(total, axis=1, keepdims=True) * (1.0 / (blocks * tile))
        inv_rms = lax.rsqrt(mean + EPSILON)
        for r in range(blocks):
            v = x_ref[0, :, columns(r, tile)].astype(F32)
            hid_ref[0, r] = ((v * inv_rms) * gain[:, columns(r, tile)]).astype(BF16)
        pre_ref[...] = jnp.zeros_like(pre_ref)

    @pl.when(live)
    def _():
        for i in range(ROWS_PER_STEP):
            r = step * ROWS_PER_STEP + i
            wide = jnp.concatenate([tiles[i * KEEP + j] for j in range(KEEP)], axis=1)
            parts = jnp.dot(hid_ref[0, r], wide, preferred_element_type=F32)
            for j in range(KEEP):
                c = cols[r * KEEP + j]
                pre_ref[0, c] += parts[:, j * tile : (j + 1) * tile]

    @pl.when(jnp.logical_and(live, step == pl.num_programs(0) - 1))
    def _():
        for r in range(blocks):
            v = x_ref[0, :, columns(r, tile)].astype(F32)
            p = pre_ref[0, r]
            y = (v + p * sigmoid(p)).astype(BF16)
            y_ref[:, columns(r, tile)] = y
            out_ref[0, :, columns(r, tile)] = y


def slot_block(shape):
    return pl.BlockSpec((1, *shape), lambda s, state, cols: (state[1],) + (0,) * len(shape))


def whole_block(shape):
    return pl.BlockSpec(shape, lambda s, state, cols: (0,) * len(shape))


def micro_block(shape):
    return pl.BlockSpec((1, *shape), lambda s, state, cols: (state[3],) + (0,) * len(shape))


def tile_block(tile):
    return pl.BlockSpec(
        (ROWS_PER_STEP * KEEP, tile, tile), lambda s, state, cols: (s, 0, 0)
    )


def run_forward(state, cols, acts, received, gain, gathered, kept):
    micros, rows, width = acts.shape
    tile = gathered.shape[1]
    blocks = width // tile
    flat, cut = (rows, width), (blocks, rows, tile)
    old = [] if kept is None else list(kept)
    return pl.pallas_call(
        forward_kernel,
        grid_spec=pltpu.PrefetchScalarGridSpec(
            num_scalar_prefetch=2,
            grid=(blocks // ROWS_PER_STEP,),
            in_specs=[
                micro_block(flat),
                whole_block(flat),
                whole_block((1, width)),
                tile_block(tile),
            ]
            + [pl.BlockSpec(memory_space=pl.ANY)] * len(old),
            out_specs=[
                whole_block(flat),
                slot_block(flat),
                slot_block(flat),
                slot_block(cut),
                slot_block(cut),
            ],
        ),
        out_shape=[
            jax.ShapeDtypeStruct(flat, BF16),
            jax.ShapeDtypeStruct((micros + 1, *flat), BF16),
            jax.ShapeDtypeStruct((micros + 1, *flat), BF16),
            jax.ShapeDtypeStruct((micros + 1, *cut), F32),
            jax.ShapeDtypeStruct((micros + 1, *cut), BF16),
        ],
        input_output_aliases={6 + i: 1 + i for i in range(len(old))},
        compiler_params=pltpu.CompilerParams(vmem_limit_bytes=VMEM_BYTES),
        cost_estimate=pl.CostEstimate(
            flops=2 * rows * KEEP * width * tile,
            bytes_accessed=gathered.size * 2,
            transcendentals=rows * width,
        ),
        name="section_forward",
    )(state, cols, acts, received, gain, gathered, *old)


def backward_kernel(state, cols, cot, received, gain, tiles, x_in, pre_in, *refs):
    g_ref, grad_ref, pd_ref, gained_ref, g_all, inv_ref, dot_ref = refs[-7:]
    blocks, rows, tile = pre_in.shape[1:]
    step = pl.program_id(0)
    live = state[0] > 0
    last = state[2] > 0

    @pl.when(jnp.logical_and(live, step == 0))
    def _():
        @pl.when(last)
        def _():
            place = lax.broadcasted_iota(jnp.int32, (rows, tile), 0)
            valid = (place < state[4]).astype(F32)
            for r in range(blocks):
                g_all[r] = (cot[0, :, columns(r, tile)].astype(F32) * valid).astype(BF16)

        @pl.when(jnp.logical_not(last))
        def _():
            for r in range(blocks):
                g_all[r] = received[:, columns(r, tile)]

        total = jnp.zeros((rows, tile), F32)
        for r in range(blocks):
            p = pre_in[0, r]
            s = sigmoid(p)
            g = g_all[r].astype(F32)
            pd_ref[0, r] = (g * s * (1.0 + p * (1.0 - s))).astype(BF16)
            v = x_in[0, :, columns(r, tile)].astype(F32)
            total = total + v * v
        mean = jnp.sum(total, axis=1, keepdims=True) * (1.0 / (blocks * tile))
        inv_ref[...] = jnp.broadcast_to(lax.rsqrt(mean + EPSILON), inv_ref.shape)
        dot_ref[...] = jnp.zeros_like(dot_ref)

    @pl.when(live)
    def _():
        for i in range(ROWS_PER_STEP):
            r = step * ROWS_PER_STEP + i
            wide = jnp.concatenate([tiles[i * KEEP + j] for j in range(KEEP)], axis=1)
            picked = jnp.concatenate(
                [pd_ref[0, cols[r * KEEP + j]] for j in range(KEEP)], axis=1
            )
            delta = lax.dot_general(
                picked, wide, (((1,), (1,)), ((), ())), preferred_element_type=F32
            )
            here = pl.ds(pl.multiple_of(r * tile, tile), tile)
            gained = delta * gain[:, here]
            gained_ref[r] = gained
            unit = x_in[0, :, here].astype(F32) * inv_ref[...]
            dot_ref[...] += gained * unit

    @pl.when(jnp.logical_and(live, step == pl.num_programs(0) - 1))
    def _():
        mean = jnp.sum(dot_ref[...], axis=1, keepdims=True) * (1.0 / (blocks * tile))
        inv = inv_ref[...]
        for r in range(blocks):
            unit = x_in[0, :, columns(r, tile)].astype(F32) * inv
            g = g_all[r].astype(F32) + inv * (gained_ref[r] - unit * mean)
            g = g.astype(BF16)
            g_ref[:, columns(r, tile)] = g
            grad_ref[0, :, columns(r, tile)] = g


def run_backward(state, cols, cot, received, gain, gathered, x_all, pre_all, kept):
    micros, rows, width = cot.shape
    tile = gathered.shape[1]
    blocks = width // tile
    flat, cut = (rows, width), (blocks, rows, tile)
    old = [] if kept is None else list(kept)
    return pl.pallas_call(
        backward_kernel,
        grid_spec=pltpu.PrefetchScalarGridSpec(
            num_scalar_prefetch=2,
            grid=(blocks // ROWS_PER_STEP,),
            in_specs=[
                micro_block(flat),
                whole_block(flat),
                whole_block((1, width)),
                tile_block(tile),
                slot_block(flat),
                slot_block(cut),
            ]
            + [pl.BlockSpec(memory_space=pl.ANY)] * len(old),
            out_specs=[whole_block(flat), slot_block(flat), slot_block(cut)],
            scratch_shapes=[
                pltpu.VMEM(cut, F32),
                pltpu.VMEM(cut, BF16),
                pltpu.VMEM((rows, tile), F32),
                pltpu.VMEM((rows, tile), F32),
            ],
        ),
        out_shape=[
            jax.ShapeDtypeStruct(flat, BF16),
            jax.ShapeDtypeStruct((micros + 1, *flat), BF16),
            jax.ShapeDtypeStruct((micros + 1, *cut), BF16),
        ],
        input_output_aliases={8 + i: 1 + i for i in range(len(old))},
        compiler_params=pltpu.CompilerParams(vmem_limit_bytes=VMEM_BYTES),
        cost_estimate=pl.CostEstimate(
            flops=2 * rows * KEEP * width * tile,
            bytes_accessed=gathered.size * 2,
            transcendentals=rows * width,
        ),
        name="section_backward",
    )(state, cols, cot, received, gain, gathered, x_all, pre_all, *old)


def tile_grad_kernel(per_group, micros, base, cols, hidden, *refs):
    deltas, out_ref = refs[:micros], refs[micros]
    share, _, _, rows, tile = hidden.shape
    start = base[0] + pl.program_id(0) * per_group
    total = None
    for m in range(micros):
        left = hidden[:, m, 0].reshape(share * rows, tile)
        right = jnp.concatenate(
            [
                deltas[m][:, cols[start + j]].reshape(share * rows, tile)
                for j in range(per_group)
            ],
            axis=1,
        )
        term = lax.dot_general(
            left, right, (((0,), (0,)), ((), ())), preferred_element_type=F32
        )
        total = term if total is None else total + term

    @pl.when(pl.program_id(1) == 0)
    def _():
        for j in range(per_group):
            out_ref[j] = total[:, j * tile : (j + 1) * tile]

    @pl.when(pl.program_id(1) > 0)
    def _():
        for j in range(per_group):
            out_ref[j] += total[:, j * tile : (j + 1) * tile]


def run_tile_grad(base, cols, hidden, deltas, tile_count):
    devices, micros, blocks, rows, tile = hidden.shape
    per_group = min(tile_count, KEEP)
    share = min(devices, 8)
    return pl.pallas_call(
        functools.partial(tile_grad_kernel, per_group, micros),
        grid_spec=pltpu.PrefetchScalarGridSpec(
            num_scalar_prefetch=2,
            grid=(tile_count // per_group, devices // share),
            in_specs=[
                pl.BlockSpec(
                    (share, micros, 1, rows, tile),
                    lambda i, k, base, cols: (k, 0, (base[0] + i * per_group) // KEEP, 0, 0),
                )
            ]
            + [
                pl.BlockSpec(
                    (share, blocks, rows, tile), lambda i, k, base, cols: (k, 0, 0, 0)
                )
            ]
            * micros,
            out_specs=pl.BlockSpec(
                (per_group, tile, tile), lambda i, k, base, cols: (i, 0, 0)
            ),
        ),
        out_shape=jax.ShapeDtypeStruct((tile_count, tile, tile), F32),
        compiler_params=pltpu.CompilerParams(vmem_limit_bytes=VMEM_BYTES),
        cost_estimate=pl.CostEstimate(
            flops=2 * tile_count * tile * tile * devices * rows * micros,
            bytes_accessed=2 * devices * micros * blocks * rows * tile,
            transcendentals=0,
        ),
        name="tile_grad",
    )(base, cols, hidden, *deltas)


def relay(value, steps):
    count = lax.axis_size("pipe")
    low, high = max(0, -steps), min(count, count - steps)
    return lax.ppermute(value, "pipe", [(i, i + steps) for i in range(low, high)])


def on_device(acts_in, cotangent, norm_gains, weights, tile_columns, lengths):
    micros, rows, width = acts_in.shape
    sections = lax.axis_size("pipe")
    here = lax.axis_index("pipe")
    cols = tile_columns[0]
    tile_count = weights.shape[1]
    gathered = lax.all_gather(weights[0], "dp", axis=0, tiled=True)
    ticks = micros + sections - 1

    def state_of(micro, special):
        live = jnp.logical_and(micro >= 0, micro < micros)
        near = jnp.clip(micro, 0, micros - 1)
        slot = jnp.where(live, near, micros)
        length = lax.dynamic_index_in_dim(lengths[:, 0], near, 0, keepdims=False)
        return jnp.stack([live.astype(jnp.int32), slot, special.astype(jnp.int32), near, length])

    received = acts_in[0]
    kept = None
    for tick in range(ticks):
        state = state_of(tick - here, here == 0)
        y, *kept = run_forward(state, cols, acts_in, received, norm_gains, gathered, kept)
        if tick < ticks - 1:
            received = relay(y, 1)
    section_out, x_all, pre_all, hid_all = kept
    hidden = lax.all_gather(hid_all[:micros], "dp", axis=0)

    received = acts_in[0]
    kept = None
    deltas = []
    for tick in range(ticks):
        state = state_of(tick - (sections - 1 - here), here == sections - 1)
        g, *kept = run_backward(
            state, cols, cotangent, received, norm_gains, gathered, x_all, pre_all, kept
        )
        if tick >= sections - 1:
            deltas.append(lax.all_gather(kept[1][tick - sections + 1], "dp", axis=0))
        if tick < ticks - 1:
            received = relay(g, -1)
    input_grad = kept[0]
    base = (lax.axis_index("dp") * tile_count).astype(jnp.int32).reshape(1)
    weight_grad = run_tile_grad(base, cols, hidden, deltas, tile_count)
    return (section_out[:micros][None], input_grad[:micros][None], weight_grad[None])


def solution(mesh):
    return jax.shard_map(
        on_device,
        mesh=mesh,
        in_specs=(
            P(None, "dp", None),
            P(None, "dp", None),
            P("pipe", None),
            P("pipe", "dp", None, None),
            P("pipe", None),
            P(None, "dp"),
        ),
        out_specs=(
            P("pipe", None, "dp", None),
            P("pipe", None, "dp", None),
            P("pipe", "dp", None, None),
        ),
        check_vma=False,
    )
```

profile of v0, /device:TPU:0, one launch (start us, length us, event | category | flops | bytes accessed | tf_op | source)
XLA Modules:
  0.0 420.9 jit_solution(14963350380402689341)
XLA Ops:
  12.3 54.7 %all-gather.11.cloned.1.call-done = bf16[1,256,128,128]{3,2,0,1:T(8,128)(2,1)} async-done(((bf16[1,32,128,128]{3,2,0,1:T(8,128)(2,1)}), bf16[1,256,128,128]{3,2,0,1:T(8,128)(2,1)}) %all-gather.11.cloned.1.call-update) | async-done | bytes 8388624 | tf_op jit(solution)/shard_map/all_gather | solution.py:321
  69.3 9.6 %section_forward.5 = (bf16[64,4096]{1,0:T(8,128)(2,1)}, bf16[3,64,4096]{2,1,0:T(8,128)(2,1)S(1)}, bf16[3,64,4096]{2,1,0:T(8,128)(2,1)S(1)}, f32[3,32,64,128]{3,2,1,0:T(8,128)}, bf16[3,32,64,128]{3,2,1,0:T(8,128)(2,1)}) custom-call(s32[5]{0:T(128)S(1)} %stack.206.state, s32[256]{0:T(256)S(1)} %bitcast.54, bf16[2,64,4096]{2,1,0:T(8,128)(2,1)S(1)} %copy-done.9, ...), custom_call_target="tpu_custom_call" | custom-call | flops 536870912 | bytes 8388608 | tf_op jit(solution)/shard_map/section_forward/pallas_call | solution.py:99
  81.7 10.6 %collective-permute-done.received = bf16[64,4096]{1,0:T(8,128)(2,1)} collective-permute-done((bf16[64,4096]{1,0:T(8,128)(2,1)}, bf16[64,4096]{1,0:T(8,128)(2,1)}, u32[]{:S(2)}, u32[]{:S(2)}) %collective-permute-start) | collective-permute-done | bytes 524320 | tf_op jit(solution)/shard_map/ppermute | solution.py:312
  93.6 9.8 %section_forward.6 = (bf16[64,4096]{1,0:T(8,128)(2,1)}, bf16[3,64,4096]{2,1,0:T(8,128)(2,1)S(1)}, bf16[3,64,4096]{2,1,0:T(8,128)(2,1)S(1)}, f32[3,32,64,128]{3,2,1,0:T(8,128)}, bf16[3,32,64,128]{3,2,1,0:T(8,128)(2,1)}) custom-call(s32[5]{0:T(128)S(1)} %stack.201.state, ...), custom_call_target="tpu_custom_call", output_to_operand_aliasing={{1}: (6, {}), {2}: (7, {}), {3}: (8, {}), {4}: (9, {})} | custom-call | flops 536870912 | bytes 8388608 | tf_op jit(solution)/shard_map/section_forward/pallas_call | solution.py:99
  103.4 5.2 %collective-permute-start.1 = (bf16[64,4096]{1,0:T(8,128)(2,1)}, bf16[64,4096]{1,0:T(8,128)(2,1)}, u32[]{:S(2)}, u32[]{:S(2)}) collective-permute-start(bf16[64,4096]{1,0:T(8,128)(2,1)} %get-tuple-element.46), channel_id=1, source_target_pairs={{0,8},{8,16},{16,24},{1,9},{9,17},{17,25},{2,10},{10,18},{18,26},{... | collective-permute-start | bytes 1572872 | tf_op jit(solution)/shard_map/ppermute | solution.py:312
  109.2 10.0 %collective-permute-done.1.received = bf16[64,4096]{1,0:T(8,128)(2,1)} collective-permute-done((bf16[64,4096]{1,0:T(8,128)(2,1)}, bf16[64,4096]{1,0:T(8,128)(2,1)}, u32[]{:S(2)}, u32[]{:S(2)}) %collective-permute-start.1) | collective-permute-done | bytes 524320 | tf_op jit(solution)/shard_map/ppermute | solution.py:312
  120.4 7.4 %section_forward.7 = (bf16[64,4096]{1,0:T(8,128)(2,1)}, bf16[3,64,4096]{2,1,0:T(8,128)(2,1)S(1)}, bf16[3,64,4096]{2,1,0:T(8,128)(2,1)S(1)}, f32[3,32,64,128]{3,2,1,0:T(8,128)}, bf16[3,32,64,128]{3,2,1,0:T(8,128)(2,1)}) custom-call(s32[5]{0:T(128)S(1)} %stack.196.state, ...), custom_call_target="tpu_custom_call", output_to_operand_aliasing={{1}: (6, {}), {2}: (7, {}), {3}: (8, {}), {4}: (9, {})} | custom-call | flops 536870912 | bytes 8388608 | tf_op jit(solution)/shard_map/section_forward/pallas_call | solution.py:99
  127.8 7.5 %collective-permute-start.2 = (bf16[64,4096]{1,0:T(8,128)(2,1)}, bf16[64,4096]{1,0:T(8,128)(2,1)}, u32[]{:S(2)}, u32[]{:S(2)}) collective-permute-start(bf16[64,4096]{1,0:T(8,128)(2,1)} %get-tuple-element.51), channel_id=1, source_target_pairs={{0,8},{8,16},{16,24},{1,9},{9,17},{17,25},{2,10},{10,18},{18,26},{... | collective-permute-start | bytes 1572872 | tf_op jit(solution)/shard_map/ppermute | solution.py:312
  136.1 9.0 %collective-permute-done.2.received = bf16[64,4096]{1,0:T(8,128)(2,1)} collective-permute-done((bf16[64,4096]{1,0:T(8,128)(2,1)}, bf16[64,4096]{1,0:T(8,128)(2,1)}, u32[]{:S(2)}, u32[]{:S(2)}) %collective-permute-start.2) | collective-permute-done | bytes 524320 | tf_op jit(solution)/shard_map/ppermute | solution.py:312
  146.3 7.4 %section_forward.8 = (bf16[64,4096]{1,0:T(8,128)(2,1)}, bf16[3,64,4096]{2,1,0:T(8,128)(2,1)S(1)}, bf16[3,64,4096]{2,1,0:T(8,128)(2,1)S(1)}, f32[3,32,64,128]{3,2,1,0:T(8,128)}, bf16[3,32,64,128]{3,2,1,0:T(8,128)(2,1)}) custom-call(s32[5]{0:T(128)S(1)} %stack.191.state, ...), custom_call_target="tpu_custom_call", output_to_operand_aliasing={{1}: (6, {}), {2}: (7, {}), {3}: (8, {}), {4}: (9, {})} | custom-call | flops 536870912 | bytes 8388608 | tf_op jit(solution)/shard_map/section_forward/pallas_call | solution.py:99
  160.3 7.3 %collective-permute-done.3.received = bf16[64,4096]{1,0:T(8,128)(2,1)} collective-permute-done((bf16[64,4096]{1,0:T(8,128)(2,1)}, bf16[64,4096]{1,0:T(8,128)(2,1)}, u32[]{:S(2)}, u32[]{:S(2)}) %collective-permute-start.3) | collective-permute-done | bytes 524320 | tf_op jit(solution)/shard_map/ppermute | solution.py:312
  168.9 7.4 %section_forward.9 = (bf16[64,4096]{1,0:T(8,128)(2,1)}, bf16[3,64,4096]{2,1,0:T(8,128)(2,1)S(1)}, bf16[3,64,4096]{2,1,0:T(8,128)(2,1)S(1)}, f32[3,32,64,128]{3,2,1,0:T(8,128)}, bf16[3,32,64,128]{3,2,1,0:T(8,128)(2,1)}) custom-call(s32[5]{0:T(128)S(1)} %stack.186.state, ...), custom_call_target="tpu_custom_call", output_to_operand_aliasing={{1}: (6, {}), {2}: (7, {}), {3}: (8, {}), {4}: (9, {})} | custom-call | flops 536870912 | bytes 8388608 | tf_op jit(solution)/shard_map/section_forward/pallas_call | solution.py:99
  177.5 7.3 %section_backward.5 = (bf16[64,4096]{1,0:T(8,128)(2,1)}, bf16[3,64,4096]{2,1,0:T(8,128)(2,1)S(1)}, bf16[3,32,64,128]{3,2,1,0:T(8,128)(2,1)S(1)}) custom-call(s32[5]{0:T(128)S(1)} %stack.233.state, s32[256]{0:T(256)S(1)} %bitcast.59, bf16[2,64,4096]{2,1,0:T(8,128)(2,1)S(1)} %copy-done.14, bf16[64,4096]{1,0:T(8,128)(2,1)S(1)} %copy-done.20, ...), custom_call_target="tpu_custom_call" | custom-call | flops 536870912 | bytes 8388608 | tf_op jit(solution)/shard_map/section_backward/pallas_call | solution.py:205
  188.0 12.9 %collective-permute-done.4.received = bf16[64,4096]{1,0:T(8,128)(2,1)} collective-permute-done((bf16[64,4096]{1,0:T(8,128)(2,1)}, bf16[64,4096]{1,0:T(8,128)(2,1)}, u32[]{:S(2)}, u32[]{:S(2)}) %collective-permute-start.4) | collective-permute-done | bytes 524320 | tf_op jit(solution)/shard_map/ppermute | solution.py:312
  203.5 7.4 %section_backward.6 = (bf16[64,4096]{1,0:T(8,128)(2,1)}, bf16[3,64,4096]{2,1,0:T(8,128)(2,1)S(1)}, bf16[3,32,64,128]{3,2,1,0:T(8,128)(2,1)S(1)}) custom-call(s32[5]{0:T(128)S(1)} %stack.228.state, s32[256]{0:T(256)S(1)} %bitcast.60, bf16[2,64,4096]{2,1,0:T(8,128)(2,1)S(1)} %copy-done.15, ...), custom_call_target="tpu_custom_call", output_to_operand_aliasing={{1}: (8, {}), {2}: (9, {})} | custom-call | flops 536870912 | bytes 8388608 | tf_op jit(solution)/shard_map/section_backward/pallas_call | solution.py:205
  214.1 11.5 %collective-permute-done.5.received = bf16[64,4096]{1,0:T(8,128)(2,1)} collective-permute-done((bf16[64,4096]{1,0:T(8,128)(2,1)}, bf16[64,4096]{1,0:T(8,128)(2,1)}, u32[]{:S(2)}, u32[]{:S(2)}) %collective-permute-start.5) | collective-permute-done | bytes 524320 | tf_op jit(solution)/shard_map/ppermute | solution.py:312
  228.2 7.4 %section_backward.7 = (bf16[64,4096]{1,0:T(8,128)(2,1)}, bf16[3,64,4096]{2,1,0:T(8,128)(2,1)S(1)}, bf16[3,32,64,128]{3,2,1,0:T(8,128)(2,1)S(1)}) custom-call(s32[5]{0:T(128)S(1)} %stack.223.state, s32[256]{0:T(256)S(1)} %bitcast.61, bf16[2,64,4096]{2,1,0:T(8,128)(2,1)S(1)} %copy-done.16, ...), custom_call_target="tpu_custom_call", output_to_operand_aliasing={{1}: (8, {}), {2}: (9, {})} | custom-call | flops 536870912 | bytes 8388608 | tf_op jit(solution)/shard_map/section_backward/pallas_call | solution.py:205
  239.0 21.1 %collective-permute-done.6.received = bf16[64,4096]{1,0:T(8,128)(2,1)} collective-permute-done((bf16[64,4096]{1,0:T(8,128)(2,1)}, bf16[64,4096]{1,0:T(8,128)(2,1)}, u32[]{:S(2)}, u32[]{:S(2)}) %collective-permute-start.6) | collective-permute-done | bytes 524320 | tf_op jit(solution)/shard_map/ppermute | solution.py:312
  262.8 9.9 %section_backward.8 = (bf16[64,4096]{1,0:T(8,128)(2,1)S(1)}, bf16[3,64,4096]{2,1,0:T(8,128)(2,1)S(1)}, bf16[3,32,64,128]{3,2,1,0:T(8,128)(2,1)S(1)}) custom-call(s32[5]{0:T(128)S(1)} %stack.218.state, s32[256]{0:T(256)S(1)} %bitcast.62, bf16[2,64,4096]{2,1,0:T(8,128)(2,1)S(1)} %copy-done.17, ...), custom_call_target="tpu_custom_call", output_to_operand_aliasing={{1}: (8, {}), {2}: (9, {})} | custom-call | flops 536870912 | bytes 8388608 | tf_op jit(solution)/shard_map/section_backward/pallas_call | solution.py:205
  277.5 9.7 %collective-permute-done.7.received = bf16[64,4096]{1,0:T(8,128)(2,1)} collective-permute-done((bf16[64,4096]{1,0:T(8,128)(2,1)}, bf16[64,4096]{1,0:T(8,128)(2,1)}, u32[]{:S(2)}, u32[]{:S(2)}) %collective-permute-start.7) | collective-permute-done | bytes 524320 | tf_op jit(solution)/shard_map/ppermute | solution.py:312
  289.9 11.0 %section_backward.9 = (bf16[64,4096]{1,0:T(8,128)(2,1)}, bf16[3,64,4096]{2,1,0:T(8,128)(2,1)S(1)}, bf16[3,32,64,128]{3,2,1,0:T(8,128)(2,1)S(1)}) custom-call(s32[5]{0:T(128)S(1)} %stack.213.state, s32[256]{0:T(256)S(1)} %bitcast.63, bf16[2,64,4096]{2,1,0:T(8,128)(2,1)S(1)} %copy-done.18, ...), custom_call_target="tpu_custom_call", output_to_operand_aliasing={{1}: (8, {}), {2}: (9, {})} | custom-call | flops 536870912 | bytes 8388608 | tf_op jit(solution)/shard_map/section_backward/pallas_call | solution.py:205
  311.0 38.6 %all-gather.9.cloned.1.call-done.refs_1_ = bf16[8,32,64,128]{3,2,1,0:T(8,128)(2,1)} async-done(((bf16[1,32,64,128]{3,2,1,0:T(8,128)(2,1)}), bf16[8,32,64,128]{3,2,1,0:T(8,128)(2,1)}) %all-gather.9.cloned.1.call-update) | async-done | bytes 4194320 | tf_op jit(solution)/shard_map/all_gather | solution.py:350
  349.6 56.2 %all-gather.13.cloned.1.call-done = bf16[16,32,64,128]{3,2,1,0:T(8,128)(2,1)} async-done(((bf16[2,32,64,128]{3,2,1,0:T(8,128)(2,1)}), bf16[16,32,64,128]{3,2,1,0:T(8,128)(2,1)}) %all-gather.13.cloned.1.call-update) | async-done | bytes 8388624 | tf_op jit(solution)/shard_map/all_gather | solution.py:339
  408.0 6.4 %tile_grad.1 = f32[32,128,128]{2,1,0:T(8,128)} custom-call(s32[1]{0:T(128)} %bitcast.48.base, s32[256]{0:T(256)S(1)} %bitcast.64, bf16[8,2,32,64,128]{4,3,2,1,0:T(8,128)(2,1)} %bitcast.75, bf16[8,32,64,128]{3,2,1,0:T(8,128)(2,1)S(1)} %copy-done.21, bf16[8,32,64,128]{3,2,1,0:T(8,128)(2,1)} %all-gather.9.cloned.1.call-done.refs_1_), custom_call_target="tpu_custom_call" | custom-call | flops 1073741824 | bytes 8388608 | tf_op jit(solution)/shard_map/tile_grad/pallas_call | solution.py:277
  (82 shorter events, 61.5 us)
Async XLA Ops:
  7.2 59.9 %copy-start.23 = (s32[1,256]{1,0:T(1,128)S(1)}, s32[1,256]{1,0:T(1,128)}, u32[]{:S(2)}) copy-start(s32[1,256]{1,0:T(1,128)} %param.10) | copy-start | bytes 3076
  7.2 59.9 %copy-start.22 = (f32[1,4096]{1,0:T(1,128)S(1)}, f32[1,4096]{1,0:T(1,128)}, u32[]{:S(2)}) copy-start(f32[1,4096]{1,0:T(1,128)} %gain.19) | copy-start | bytes 49156
  7.2 59.8 %all-gather.11.cloned.1.call-start = ((), (), s32[]{:S(2)}) async-start(), calls=%async_computation.2 | async-start | bytes 9437184 | tf_op jit(solution)/shard_map/all_gather | solution.py:321
  7.9 303.1 %all-gather.7.cloned.1.call-start = ((), (), s32[]{:S(2)}) async-start(), calls=%async_computation | async-start | bytes 4718592 | tf_op jit(solution)/shard_map/all_gather | solution.py:350
  67.0 1.2 copy-start.9
  78.9 13.5 %collective-permute-start = (bf16[64,4096]{1,0:T(8,128)(2,1)}, bf16[64,4096]{1,0:T(8,128)(2,1)}, u32[]{:S(2)}, u32[]{:S(2)}) collective-permute-start(bf16[64,4096]{1,0:T(8,128)(2,1)} %get-tuple-element.41), channel_id=1, source_target_pairs={{0,8},{8,16},{16,24},{1,9},{9,17},{17,25},{2,10},{10,18},{18,26},{... | collective-permute-start | bytes 1572872 | tf_op jit(solution)/shard_map/ppermute | solution.py:312
  92.4 1.2 copy-start.10
  103.4 15.8 %collective-permute-start.1 = (bf16[64,4096]{1,0:T(8,128)(2,1)}, bf16[64,4096]{1,0:T(8,128)(2,1)}, u32[]{:S(2)}, u32[]{:S(2)}) collective-permute-start(bf16[64,4096]{1,0:T(8,128)(2,1)} %get-tuple-element.46), channel_id=1, source_target_pairs={{0,8},{8,16},{16,24},{1,9},{9,17},{17,25},{2,10},{10,18},{18,26},{... | collective-permute-start | bytes 1572872 | tf_op jit(solution)/shard_map/ppermute | solution.py:312
  119.2 1.2 copy-start.11
  127.8 17.2 %collective-permute-start.2 = (bf16[64,4096]{1,0:T(8,128)(2,1)}, bf16[64,4096]{1,0:T(8,128)(2,1)}, u32[]{:S(2)}, u32[]{:S(2)}) collective-permute-start(bf16[64,4096]{1,0:T(8,128)(2,1)} %get-tuple-element.51), channel_id=1, source_target_pairs={{0,8},{8,16},{16,24},{1,9},{9,17},{17,25},{2,10},{10,18},{18,26},{... | collective-permute-start | bytes 1572872 | tf_op jit(solution)/shard_map/ppermute | solution.py:312
  153.7 13.9 %collective-permute-start.3 = (bf16[64,4096]{1,0:T(8,128)(2,1)}, bf16[64,4096]{1,0:T(8,128)(2,1)}, u32[]{:S(2)}, u32[]{:S(2)}) collective-permute-start(bf16[64,4096]{1,0:T(8,128)(2,1)} %get-tuple-element.56), channel_id=1, source_target_pairs={{0,8},{8,16},{16,24},{1,9},{9,17},{17,25},{2,10},{10,18},{18,26},{... | collective-permute-start | bytes 1572872 | tf_op jit(solution)/shard_map/ppermute | solution.py:312
  168.9 8.6 %copy-start.14 = (bf16[2,64,4096]{2,1,0:T(8,128)(2,1)S(1)}, bf16[2,64,4096]{2,1,0:T(8,128)(2,1)}, u32[]{:S(2)}) copy-start(bf16[2,64,4096]{2,1,0:T(8,128)(2,1)} %cot.9) | copy-start | bytes 3145732
  168.9 8.6 %copy-start.20 = (bf16[64,4096]{1,0:T(8,128)(2,1)S(1)}, bf16[64,4096]{1,0:T(8,128)(2,1)}, u32[]{:S(2)}) copy-start(bf16[64,4096]{1,0:T(8,128)(2,1)} %slice_bitcast_fusion.2.received) | copy-start | bytes 1572868
  185.9 15.0 %collective-permute-start.4 = (bf16[64,4096]{1,0:T(8,128)(2,1)}, bf16[64,4096]{1,0:T(8,128)(2,1)}, u32[]{:S(2)}, u32[]{:S(2)}) collective-permute-start(bf16[64,4096]{1,0:T(8,128)(2,1)} %get-tuple-element.64), channel_id=1, source_target_pairs={{8,0},{16,8},{24,16},{9,1},{17,9},{25,17},{10,2},{18,10},{26,18},{... | collective-permute-start | bytes 1572872 | tf_op jit(solution)/shard_map/ppermute | solution.py:312
  200.9 1.4 copy-start.2
  212.1 13.5 %collective-permute-start.5 = (bf16[64,4096]{1,0:T(8,128)(2,1)}, bf16[64,4096]{1,0:T(8,128)(2,1)}, u32[]{:S(2)}, u32[]{:S(2)}) collective-permute-start(bf16[64,4096]{1,0:T(8,128)(2,1)} %get-tuple-element.67), channel_id=1, source_target_pairs={{8,0},{16,8},{24,16},{9,1},{17,9},{25,17},{10,2},{18,10},{26,18},{... | collective-permute-start | bytes 1572872 | tf_op jit(solution)/shard_map/ppermute | solution.py:312
  225.6 1.4 copy-start.4
  236.8 23.3 %collective-permute-start.6 = (bf16[64,4096]{1,0:T(8,128)(2,1)}, bf16[64,4096]{1,0:T(8,128)(2,1)}, u32[]{:S(2)}, u32[]{:S(2)}) collective-permute-start(bf16[64,4096]{1,0:T(8,128)(2,1)} %get-tuple-element.70), channel_id=1, source_target_pairs={{8,0},{16,8},{24,16},{9,1},{17,9},{25,17},{10,2},{18,10},{26,18},{... | collective-permute-start | bytes 1572872 | tf_op jit(solution)/shard_map/ppermute | solution.py:312
  260.1 1.4 copy-start.6
  275.5 74.2 %all-gather.9.cloned.1.call-start = ((), (), s32[]{:S(2)}) async-start(), calls=%async_computation.1 | async-start | bytes 4718592 | tf_op jit(solution)/shard_map/all_gather | solution.py:350
  275.5 11.8 %collective-permute-start.7 = (bf16[64,4096]{1,0:T(8,128)(2,1)}, bf16[64,4096]{1,0:T(8,128)(2,1)}, u32[]{:S(2)}, u32[]{:S(2)}) collective-permute-start(bf16[64,4096]{1,0:T(8,128)(2,1)} %copy-done.24), channel_id=1, source_target_pairs={{8,0},{16,8},{24,16},{9,1},{17,9},{25,17},{10,2},{18,10},{26,18},{... | collective-permute-start | bytes 1572872 | tf_op jit(solution)/shard_map/ppermute | solution.py:312
  287.3 1.4 copy-start.8
  301.8 104.0 %all-gather.13.cloned.1.call-start = ((), (), s32[]{:S(2)}) async-start(), calls=%async_computation.3 | async-start | bytes 9437184 | tf_op jit(solution)/shard_map/all_gather | solution.py:339
  405.8 2.2 copy-start.21
  (13 other events, 14.9 us)
Sparse Core Ops, SparseCore 0:
  9.9 57.0 all-gather.10
  275.6 35.3 all-gather.6
  312.9 36.7 all-gather.8
  351.4 54.3 all-gather.12
where the time goes:
time: 423 us; the launch traced here: 421 us
  waiting for transfers between devices  247 us (58%)
  Pallas kernels  91.1 us (22%)
  local copies, waits for them, and re-layouts  43.3 us (10%)
  starting transfers between devices  25.5 us (6%)
  between operations  14 us (3%)
    ppermute x8, waiting for transfers between devices, relay(): lax.ppermute(value, 'pipe', [(i, i + steps) for i in range(low, high)])  92.1 us
    all_gather x1, waiting for transfers between devices, on_device(): hidden = lax.all_gather(hid_all[:micros], 'dp', axis=0)  56.2 us
    all_gather x1, waiting for transfers between devices, on_device(): gathered = lax.all_gather(weights[0], 'dp', axis=0, tiled=True)  54.7 us
    all_gather x2, waiting for transfers between devices, on_device(): deltas.append(lax.all_gather(kept[1][tick - sections + 1], 'dp', axis=0))  43.4 us
    pallas_call x5, Pallas kernels, run_backward(): pl.pallas_call(backward_kernel, grid_spec=pltpu.PrefetchScalarGridSpec(nu...  43 us
    pallas_call x5, Pallas kernels, run_forward(): pl.pallas_call(forward_kernel, grid_spec=pltpu.PrefetchScalarGridSpec(num...  41.7 us
    unnamed x50, local copies, waits for them, and re-layouts  26.4 us
    ppermute x8, starting transfers between devices, relay(): lax.ppermute(value, 'pipe', [(i, i + steps) for i in range(low, high)])  25.3 us
  transfers between devices with their start and end apart: 12, of which 12 were waited for; matrix products, arithmetic and copies ran while one was open for 4% of the time, Pallas kernels for 3%

commit v1 on v0

v1 whole, which is shorter than its diff:
```python
import functools

import jax
import jax.numpy as jnp
from jax import lax
from jax.experimental import pallas as pl
from jax.experimental.pallas import tpu as pltpu
from jax.sharding import PartitionSpec as P

KEEP = 8
EPSILON = 1e-05
ROWS_PER_STEP = 4
SPLIT = 2
VMEM_BYTES = 48 * 1024 * 1024

F32 = jnp.float32
BF16 = jnp.bfloat16


def sigmoid(v):
    return 1.0 / (1.0 + jnp.exp(-v))


def columns(block, tile):
    return pl.ds(block * tile, tile)


def greet():
    here, count = lax.axis_index("pipe"), lax.axis_size("pipe")
    barrier = pltpu.get_barrier_semaphore()
    for other in (lax.rem(here + 1, count), lax.rem(here + count - 1, count)):
        pl.semaphore_signal(
            barrier, inc=1, device_id={"pipe": other}, device_id_type=pl.DeviceIdType.MESH
        )
    pl.semaphore_wait(barrier, 2)


def hop(source, landing, send_sems, recv_sems, chunk, target):
    return pltpu.make_async_remote_copy(
        src_ref=source.at[chunk],
        dst_ref=landing.at[chunk],
        send_sem=send_sems.at[chunk],
        recv_sem=recv_sems.at[chunk],
        device_id={"pipe": target},
        device_id_type=pl.DeviceIdType.MESH,
    )


def forward_kernel(
    order, keep, last_of, filled, acts, gain, tiles,
    out_ref, x_ref, pre_ref, hid_ref,
    landing, parts_ref, sums_ref, send_sems, recv_sems,
):
    chunks, blocks, rows, tile = pre_ref.shape
    here, count = lax.axis_index("pipe"), lax.axis_size("pipe")
    target = lax.rem(here + 1, count)
    greet()

    def one_chunk(q, carried):
        copy = hop(out_ref, landing, send_sems, recv_sems, q, target)

        @pl.when(here == 0)
        def _():
            x_ref[q] = acts[q]

        @pl.when(here > 0)
        def _():
            copy.wait_recv()
            x_ref[q] = landing[q]

        total = jnp.zeros((rows, tile), F32)
        for r in range(blocks):
            v = x_ref[q, :, columns(r, tile)].astype(F32)
            total = total + v * v
        mean = jnp.sum(total, axis=1, keepdims=True) * (1.0 / (blocks * tile))
        inv_rms = lax.rsqrt(mean + EPSILON)
        for r in range(blocks):
            v = x_ref[q, :, columns(r, tile)].astype(F32)
            hid_ref[q, r] = ((v * inv_rms) * gain[:, columns(r, tile)]).astype(BF16)

        def some_rows(s, unused):
            for i in range(ROWS_PER_STEP):
                r = s * ROWS_PER_STEP + i
                wide = jnp.concatenate([tiles[r * KEEP + j] for j in range(KEEP)], axis=1)
                parts = jnp.dot(hid_ref[q, r], wide, preferred_element_type=F32)
                for j in range(KEEP):
                    parts_ref[r * KEEP + j] = parts[:, j * tile : (j + 1) * tile]
            return unused

        lax.fori_loop(0, blocks // ROWS_PER_STEP, some_rows, 0)

        def some_sums(s, running):
            for i in range(KEEP):
                k = s * KEEP + i
                running = running * keep[k] + parts_ref[order[k]]
                sums_ref[k] = running
            return running

        lax.fori_loop(0, blocks, some_sums, jnp.zeros((rows, tile), F32))
        for r in range(blocks):
            p = sums_ref[last_of[r]] * filled[r]
            pre_ref[q, r] = p
            v = x_ref[q, :, columns(r, tile)].astype(F32)
            out_ref[q, :, columns(r, tile)] = (v + p * sigmoid(p)).astype(BF16)

        @pl.when(here < count - 1)
        def _():
            copy.start()

        return carried

    lax.fori_loop(0, chunks, one_chunk, 0)

    @pl.when(here < count - 1)
    def _():
        for q in range(chunks):
            hop(out_ref, landing, send_sems, recv_sems, q, target).wait_send()


def in_vmem(count):
    return [pl.BlockSpec(memory_space=pltpu.VMEM)] * count


def in_smem(count):
    return [pl.BlockSpec(memory_space=pltpu.SMEM)] * count


def run_forward(tables, acts, gain, gathered):
    chunks, rows, width = acts.shape
    tile_total, tile, _ = gathered.shape
    blocks = width // tile
    cut = (blocks, rows, tile)
    return pl.pallas_call(
        forward_kernel,
        in_specs=in_smem(4) + in_vmem(3),
        out_specs=in_vmem(4),
        out_shape=[
            jax.ShapeDtypeStruct(acts.shape, BF16),
            jax.ShapeDtypeStruct(acts.shape, BF16),
            jax.ShapeDtypeStruct((chunks, *cut), F32),
            jax.ShapeDtypeStruct((chunks, *cut), BF16),
        ],
        scratch_shapes=[
            pltpu.VMEM(acts.shape, BF16),
            pltpu.VMEM((tile_total, rows, tile), F32),
            pltpu.VMEM((tile_total, rows, tile), F32),
            pltpu.SemaphoreType.DMA((chunks,)),
            pltpu.SemaphoreType.DMA((chunks,)),
        ],
        compiler_params=pltpu.CompilerParams(
            vmem_limit_bytes=VMEM_BYTES, collective_id=0, has_side_effects=True
        ),
        cost_estimate=pl.CostEstimate(
            flops=2 * chunks * rows * KEEP * width * tile,
            bytes_accessed=gathered.size * 2,
            transcendentals=chunks * rows * width,
        ),
        name="forward_relay",
    )(*tables, acts, gain, gathered)


def backward_kernel(
    split, cols, lens, cot, gain, tiles, x_in, pre_in,
    grad_ref, pd_ref,
    landing, g_all, gained_ref, dot_ref, send_sems, recv_sems,
):
    chunks, blocks, rows, tile = pre_in.shape
    here, count = lax.axis_index("pipe"), lax.axis_size("pipe")
    target = lax.rem(here + count - 1, count)
    greet()

    def one_chunk(q, carried):
        copy = hop(grad_ref, landing, send_sems, recv_sems, q, target)

        @pl.when(here == count - 1)
        def _():
            start = lax.rem(q, split) * rows
            place = lax.broadcasted_iota(jnp.int32, (rows, tile), 0) + start
            valid = (place < lens[q // split]).astype(F32)
            for r in range(blocks):
                g_all[r] = (cot[q, :, columns(r, tile)].astype(F32) * valid).astype(BF16)

        @pl.when(here < count - 1)
        def _():
            copy.wait_recv()
            for r in range(blocks):
                g_all[r] = landing[q, :, columns(r, tile)]

        total = jnp.zeros((rows, tile), F32)
        for r in range(blocks):
            p = pre_in[q, r]
            s = sigmoid(p)
            g = g_all[r].astype(F32)
            pd_ref[q, r] = (g * s * (1.0 + p * (1.0 - s))).astype(BF16)
            v = x_in[q, :, columns(r, tile)].astype(F32)
            total = total + v * v
        mean = jnp.sum(total, axis=1, keepdims=True) * (1.0 / (blocks * tile))
        inv = jnp.broadcast_to(lax.rsqrt(mean + EPSILON), (rows, tile))
        dot_ref[...] = jnp.zeros_like(dot_ref)

        def some_rows(s, unused):
            for i in range(ROWS_PER_STEP):
                r = s * ROWS_PER_STEP + i
                wide = jnp.concatenate([tiles[r * KEEP + j] for j in range(KEEP)], axis=1)
                picked = jnp.concatenate(
                    [pd_ref[q, cols[r * KEEP + j]] for j in range(KEEP)], axis=1
                )
                delta = lax.dot_general(
                    picked, wide, (((1,), (1,)), ((), ())), preferred_element_type=F32
                )
                at = pl.ds(pl.multiple_of(r * tile, tile), tile)
                gained = delta * gain[:, at]
                gained_ref[r] = gained
                dot_ref[...] += gained * (x_in[q, :, at].astype(F32) * inv)
            return unused

        lax.fori_loop(0, blocks // ROWS_PER_STEP, some_rows, 0)
        mean = jnp.sum(dot_ref[...], axis=1, keepdims=True) * (1.0 / (blocks * tile))
        for r in range(blocks):
            unit = x_in[q, :, columns(r, tile)].astype(F32) * inv
            g = g_all[r].astype(F32) + inv * (gained_ref[r] - unit * mean)
            grad_ref[q, :, columns(r, tile)] = g.astype(BF16)

        @pl.when(here > 0)
        def _():
            copy.start()

        return carried

    lax.fori_loop(0, chunks, one_chunk, 0)

    @pl.when(here > 0)
    def _():
        for q in range(chunks):
            hop(grad_ref, landing, send_sems, recv_sems, q, target).wait_send()


def run_backward(split, cols, lens, cot, gain, gathered, x_all, pre_all):
    chunks, rows, width = cot.shape
    tile = gathered.shape[1]
    cut = (width // tile, rows, tile)
    return pl.pallas_call(
        functools.partial(backward_kernel, split),
        in_specs=in_smem(2) + in_vmem(5),
        out_specs=in_vmem(2),
        out_shape=[
            jax.ShapeDtypeStruct(cot.shape, BF16),
            jax.ShapeDtypeStruct((chunks, *cut), BF16),
        ],
        scratch_shapes=[
            pltpu.VMEM(cot.shape, BF16),
            pltpu.VMEM(cut, BF16),
            pltpu.VMEM(cut, F32),
            pltpu.VMEM((rows, tile), F32),
            pltpu.SemaphoreType.DMA((chunks,)),
            pltpu.SemaphoreType.DMA((chunks,)),
        ],
        compiler_params=pltpu.CompilerParams(
            vmem_limit_bytes=VMEM_BYTES, collective_id=1, has_side_effects=True
        ),
        cost_estimate=pl.CostEstimate(
            flops=2 * chunks * rows * KEEP * width * tile,
            bytes_accessed=gathered.size * 2,
            transcendentals=chunks * rows * width,
        ),
        name="backward_relay",
    )(cols, lens, cot, gain, gathered, x_all, pre_all)


def tile_grad_kernel(per_group, base, cols, hidden, deltas, out_ref):
    share, micros, _, rows, tile = hidden.shape
    start = base[0] + pl.program_id(0) * per_group
    total = None
    for m in range(micros):
        left = hidden[:, m, 0].reshape(share * rows, tile)
        right = jnp.concatenate(
            [
                deltas[:, m, cols[start + j]].reshape(share * rows, tile)
                for j in range(per_group)
            ],
            axis=1,
        )
        term = lax.dot_general(
            left, right, (((0,), (0,)), ((), ())), preferred_element_type=F32
        )
        total = term if total is None else total + term

    @pl.when(pl.program_id(1) == 0)
    def _():
        for j in range(per_group):
            out_ref[j] = total[:, j * tile : (j + 1) * tile]

    @pl.when(pl.program_id(1) > 0)
    def _():
        for j in range(per_group):
            out_ref[j] += total[:, j * tile : (j + 1) * tile]


def run_tile_grad(base, cols, hidden, deltas, tile_count):
    devices, micros, blocks, rows, tile = hidden.shape
    per_group = min(tile_count, KEEP)
    share = min(devices, 8)
    return pl.pallas_call(
        functools.partial(tile_grad_kernel, per_group),
        grid_spec=pltpu.PrefetchScalarGridSpec(
            num_scalar_prefetch=2,
            grid=(tile_count // per_group, devices // share),
            in_specs=[
                pl.BlockSpec(
                    (share, micros, 1, rows, tile),
                    lambda i, k, base, cols: (k, 0, (base[0] + i * per_group) // KEEP, 0, 0),
                )
            ]
            + [
                pl.BlockSpec(
                    (share, micros, blocks, rows, tile),
                    lambda i, k, base, cols: (k, 0, 0, 0, 0),
                )
            ],
            out_specs=pl.BlockSpec(
                (per_group, tile, tile), lambda i, k, base, cols: (i, 0, 0)
            ),
        ),
        out_shape=jax.ShapeDtypeStruct((tile_count, tile, tile), F32),
        compiler_params=pltpu.CompilerParams(vmem_limit_bytes=VMEM_BYTES),
        cost_estimate=pl.CostEstimate(
            flops=2 * tile_count * tile * tile * devices * rows * micros,
            bytes_accessed=2 * devices * micros * blocks * rows * tile,
            transcendentals=0,
        ),
        name="tile_grad",
    )(base, cols, hidden, deltas)


def column_order(cols, blocks):
    spots = jnp.arange(cols.shape[0], dtype=jnp.int32)
    before = jnp.logical_or(
        cols[None, :] < cols[:, None],
        jnp.logical_and(cols[None, :] == cols[:, None], spots[None, :] < spots[:, None]),
    )
    rank = jnp.sum(before.astype(jnp.int32), axis=1)
    hit = (rank[None, :] == spots[:, None]).astype(jnp.int32)
    order = jnp.sum(hit * spots[None, :], axis=1)
    column = jnp.sum(hit * cols[None, :], axis=1)
    same = jnp.concatenate([jnp.zeros((1,), jnp.bool_), column[1:] == column[:-1]])
    blocks_at = jnp.arange(blocks, dtype=jnp.int32)[:, None]
    upto = jnp.sum((cols[None, :] <= blocks_at).astype(jnp.int32), axis=1)
    own = jnp.sum((cols[None, :] == blocks_at).astype(jnp.int32), axis=1)
    return order, same.astype(F32), jnp.maximum(upto - 1, 0), (own > 0).astype(F32)


def on_device(acts_in, cotangent, norm_gains, weights, tile_columns, lengths):
    micros, rows, width = acts_in.shape
    cols = tile_columns[0]
    tile_count, tile = weights.shape[1:3]
    chunks = (micros * SPLIT, rows // SPLIT, width)
    gathered = lax.all_gather(weights[0], "dp", axis=0, tiled=True)
    tables = column_order(cols, width // tile)
    section_out, x_all, pre_all, hid_all = run_forward(
        tables, acts_in.reshape(chunks), norm_gains, gathered
    )
    hidden = lax.all_gather(hid_all, "dp", axis=0)
    input_grad, pd_all = run_backward(
        SPLIT, cols, lengths[:, 0], cotangent.reshape(chunks), norm_gains, gathered, x_all, pre_all
    )
    hidden, pd_all = lax.optimization_barrier((hidden, pd_all))
    deltas = lax.all_gather(pd_all, "dp", axis=0)
    base = (lax.axis_index("dp") * tile_count).astype(jnp.int32).reshape(1)
    weight_grad = run_tile_grad(base, cols, hidden, deltas, tile_count)
    whole = acts_in.shape
    return (section_out.reshape(whole)[None], input_grad.reshape(whole)[None], weight_grad[None])


def solution(mesh):
    return jax.shard_map(
        on_device,
        mesh=mesh,
        in_specs=(
            P(None, "dp", None),
            P(None, "dp", None),
            P("pipe", None),
            P("pipe", "dp", None, None),
            P("pipe", None),
            P(None, "dp"),
        ),
        out_specs=(
            P("pipe", None, "dp", None),
            P("pipe", None, "dp", None),
            P("pipe", "dp", None, None),
        ),
        check_vma=False,
    )
```

time: 423 us -> 255 us (0.60)
  waiting for transfers between devices: 247 us -> 109 us
  local copies, waits for them, and re-layouts: 43.3 us -> 6.8 us
  Pallas kernels: 91.1 us -> 123 us
  starting transfers between devices: 25.5 us -> 0.12 us
    ppermute x8 -> x0, waiting for transfers between devices: 92.1 us -> none  [relay(): lax.ppermute(value, 'pipe', [(i, i + steps) for i in range(low, high)])]
    all_gather x3 -> x2, waiting for transfers between devices: 99.5 us -> 51.8 us  [the longest x1 51.8 us: on_device(): deltas = lax.all_gather(pd_all, 'dp', axis=0)]
    pallas_call x11 -> x3, Pallas kernels: 91.1 us -> 123 us  [the longest x1 80.7 us: run_backward(): pl.pallas_call(functools.partial(backward_kernel, split), in_specs=in_sme...]
    ppermute x8 -> x0, starting transfers between devices: 25.3 us -> none  [relay(): lax.ppermute(value, 'pipe', [(i, i + steps) for i in range(low, high)])]
    unnamed x50 -> x22, local copies, waits for them, and re-layouts: 26.4 us -> 6.8 us
    another operation x10 -> x0, local copies, waits for them, and re-layouts: 7.22 us -> none  [state_of(): jnp.stack([live.astype(jnp.int32), slot, special.astype(jnp.int32), near,...]
  transfers between devices with their start and end apart: 12 -> 3, of which waited for: 12 -> 2; matrix products, arithmetic and copies ran while one was open for 4% -> 1% of each run, Pallas kernels for 3% -> 32%
where the time goes in v1:
time: 255 us
  Pallas kernels  123 us (48%)
  waiting for transfers between devices  109 us (43%)
  between operations  13.9 us (5%)
  local copies, waits for them, and re-layouts  6.8 us (3%)
  other arithmetic  2.74 us (1%)
    pallas_call x1, Pallas kernels, run_backward(): pl.pallas_call(functools.partial(backward_kernel, split), in_specs=in_sme...  80.7 us
    all_gather x1, waiting for transfers between devices, on_device(): gathered = lax.all_gather(weights[0], 'dp', axis=0, tiled=True)  56.3 us
    all_gather x1, waiting for transfers between devices, on_device(): deltas = lax.all_gather(pd_all, 'dp', axis=0)  51.8 us
    pallas_call x1, Pallas kernels, run_forward(): pl.pallas_call(forward_kernel, in_specs=in_smem(4) + in_vmem(3), out_spec...  34.3 us
    pallas_call x1, Pallas kernels, run_tile_grad(): pl.pallas_call(functools.partial(tile_grad_kernel, per_group), grid_spec=...  7.59 us
    unnamed x22, local copies, waits for them, and re-layouts  6.8 us
  transfers between devices with their start and end apart: 3, of which 2 were waited for; matrix products, arithmetic and copies ran while one was open for 1% of the time, Pallas kernels for 32%

profile of v1, /device:TPU:0, one launch (start us, length us, event | category | flops | bytes accessed | tf_op | source)
XLA Modules:
  0.0 255.0 jit_solution(8611190789248327419)
XLA Ops:
  7.2 0.0 all-gather.7.cloned.1.call-start
  7.3 0.7 all-gather.7.cloned.1.call-update
  7.9 0.0 all-gather.9.cloned.1.call-start
  8.0 0.9 convert_reduce_fusion
  8.9 0.8 select_reduce_fusion
  9.8 0.1 slice_compare_fusion
  9.8 0.1 add_convert_fusion.keep
  9.9 0.8 convert_reduce_fusion.1
  10.7 56.3 %all-gather.7.cloned.1.call-done = bf16[1,256,128,128]{3,2,0,1:T(8,128)(2,1)} async-done(((bf16[1,32,128,128]{3,2,0,1:T(8,128)(2,1)}), bf16[1,256,128,128]{3,2,0,1:T(8,128)(2,1)}) %all-gather.7.cloned.1.call-update) | async-done | bytes 8388624 | tf_op jit(solution)/shard_map/all_gather | solution.py:357
  67.1 1.2 copy-done.5
  68.3 0.7 copy-done.6
  69.0 34.3 %forward_relay.1 = (bf16[4,32,4096]{2,1,0:T(8,128)(2,1)S(1)}, bf16[4,32,4096]{2,1,0:T(8,128)(2,1)S(1)}, f32[4,32,32,128]{3,2,1,0:T(8,128)}, bf16[4,32,32,128]{3,2,1,0:T(8,128)(2,1)S(1)}) custom-call(s32[256]{0:T(256)S(1)} %get-tuple-element.22.order, f32[256]{0:T(256)S(1)} %add_convert_fusion.keep, s32[32]{0:T(128)S(1)} %add_maximum_fusion.last_of, ...), custom_call_target="tpu_custom_call" | custom-call | flops 1073741824 | bytes 8388608 | tf_op jit(solution)/shard_map/forward_relay/pallas_call | solution.py:133
  103.3 0.0 copy-start.4
  103.3 1.0 copy-done.4
  104.3 0.0 all-gather.9.cloned.1.call-update
  104.3 0.0 all-gather.11.cloned.1.call-start
  104.4 80.7 %backward_relay.1 = (bf16[4,32,4096]{2,1,0:T(8,128)(2,1)S(1)}, bf16[4,32,32,128]{3,2,1,0:T(8,128)(2,1)S(1)}) custom-call(s32[256]{0:T(256)S(1)} %bitcast.19, s32[2]{0:T(128)S(1)} %bitcast.21, bf16[4,32,4096]{2,1,0:T(8,128)(2,1)S(1)} %bitcast.12, f32[1,4096]{1,0:T(1,128)S(1)} %copy-done.7, bf16[256,128,128]{2,1,0:T(8,128)(2,1)} %bitcast.23, ...), custom_call_target="tpu_custom_call" | custom-call | flops 1073741824 | bytes 8388608 | tf_op jit(solution)/shard_map/backward_relay/pallas_call | solution.py:242
  185.1 1.0 copy-done.1
  186.1 1.0 copy-done.3
  187.1 0.0 all-gather.11.cloned.1.call-update
  187.1 51.8 %all-gather.11.cloned.1.call-done = bf16[32,32,32,128]{3,2,1,0:T(8,128)(2,1)} async-done(((bf16[4,32,32,128]{3,2,1,0:T(8,128)(2,1)}), bf16[32,32,32,128]{3,2,1,0:T(8,128)(2,1)}) %all-gather.11.cloned.1.call-update) | async-done | bytes 8388624 | tf_op jit(solution)/shard_map/all_gather | solution.py:367
  238.9 7.6 %tile_grad.1 = f32[32,128,128]{2,1,0:T(8,128)} custom-call(s32[1]{0:T(128)} %bitcast.8.base, s32[256]{0:T(256)S(1)} %bitcast.20, bf16[8,4,32,32,128]{4,3,2,1,0:T(8,128)(2,1)} %bitcast.24, bf16[8,4,32,32,128]{4,3,2,1,0:T(8,128)(2,1)} %bitcast.25), custom_call_target="tpu_custom_call" | custom-call | flops 1073741824 | bytes 8388608 | tf_op jit(solution)/shard_map/tile_grad/pallas_call | solution.py:303
  246.5 1.0 copy.13
  247.5 1.0 copy.14
  (17 shorter events, 0.0 us)
Async XLA Ops:
  7.2 97.2 %copy-start.8 = (s32[1,256]{1,0:T(1,128)S(1)}, s32[1,256]{1,0:T(1,128)}, u32[]{:S(2)}) copy-start(s32[1,256]{1,0:T(1,128)} %param.10) | copy-start | bytes 3076
  7.2 97.2 %copy-start.7 = (f32[1,4096]{1,0:T(1,128)S(1)}, f32[1,4096]{1,0:T(1,128)}, u32[]{:S(2)}) copy-start(f32[1,4096]{1,0:T(1,128)} %gain.3) | copy-start | bytes 49156
  7.2 97.2 %copy-start.9 = (s32[2,1]{0,1:T(1,128)S(1)}, s32[2,1]{0,1:T(1,128)}, u32[]{:S(2)}) copy-start(s32[2,1]{0,1:T(1,128)} %param.11) | copy-start | bytes 28
  7.2 97.2 %copy-start = (bf16[2,64,4096]{2,1,0:T(8,128)(2,1)S(1)}, bf16[2,64,4096]{2,1,0:T(8,128)(2,1)}, u32[]{:S(2)}) copy-start(bf16[2,64,4096]{2,1,0:T(8,128)(2,1)} %param.7) | copy-start | bytes 3145732
  7.2 59.8 %all-gather.7.cloned.1.call-start = ((), (), s32[]{:S(2)}) async-start(), calls=%async_computation | async-start | bytes 9437184 | tf_op jit(solution)/shard_map/all_gather | solution.py:357
  7.9 179.1 %all-gather.9.cloned.1.call-start = ((), (), s32[]{:S(2)}) async-start(), calls=%async_computation.1 | async-start | bytes 9437184 | tf_op jit(solution)/shard_map/all_gather | solution.py:362
  67.1 1.2 copy-start.5
  68.3 0.7 copy-start.6
  103.3 1.0 copy-start.4
  104.3 134.6 %all-gather.11.cloned.1.call-start = ((), (), s32[]{:S(2)}) async-start(), calls=%async_computation.2 | async-start | bytes 9437184 | tf_op jit(solution)/shard_map/all_gather | solution.py:367
  185.1 1.0 copy-start.1
  186.1 1.0 copy-start.3
  238.9 8.6 %copy-start.2 = (bf16[4,32,4096]{2,1,0:T(8,128)(2,1)S(1)}, bf16[4,32,4096]{2,1,0:T(8,128)(2,1)}, u32[]{:S(2)}) copy-start(bf16[4,32,4096]{2,1,0:T(8,128)(2,1)} %copy-done.1) | copy-start | bytes 3145732
Sparse Core Ops, SparseCore 0:
  9.9 57.0 all-gather.6
  104.4 77.5 all-gather.8
  187.2 51.6 all-gather.10

commit v2 on v1

--- a/solution.py
+++ b/solution.py
@@ -25,14 +25,27 @@
     return pl.ds(block * tile, tile)
 
 
-def greet():
+def greet(sharers=1):
     here, count = lax.axis_index("pipe"), lax.axis_size("pipe")
     barrier = pltpu.get_barrier_semaphore()
+    me = lax.axis_index("dp")
+
+    def one_sharer(j, unused):
+        pl.semaphore_signal(
+            barrier,
+            inc=1,
+            device_id={"dp": lax.rem(me + j, sharers)},
+            device_id_type=pl.DeviceIdType.MESH,
+        )
+        return unused
+
+    if sharers > 1:
+        lax.fori_loop(1, sharers, one_sharer, 0)
     for other in (lax.rem(here + 1, count), lax.rem(here + count - 1, count)):
         pl.semaphore_signal(
             barrier, inc=1, device_id={"pipe": other}, device_id_type=pl.DeviceIdType.MESH
         )
-    pl.semaphore_wait(barrier, 2)
+    pl.semaphore_wait(barrier, sharers + 1)
 
 
 def hop(source, landing, send_sems, recv_sems, chunk, target):
@@ -46,6 +59,85 @@
     )
 
 
+def to_sharer(source, landing, send_sem, recv_sem, target):
+    return pltpu.make_async_remote_copy(
+        src_ref=source,
+        dst_ref=landing,
+        send_sem=send_sem,
+        recv_sem=recv_sem,
+        device_id={"dp": target},
+        device_id_type=pl.DeviceIdType.MESH,
+    )
+
+
+class Exchange:
+    def __init__(self, source, landing, out_sems, in_sems, pair_out, pair_in, own_sem):
+        self.source, self.landing, self.own_sem = source, landing, own_sem
+        self.out_sems, self.in_sems = out_sems, in_sems
+        self.pair_out, self.pair_in = pair_out, pair_in
+        self.me = lax.axis_index("dp")
+        self.chips = lax.axis_size("dp") // 2
+        self.chip, self.core = self.me // 2, lax.rem(self.me, 2)
+        self.sibling = self.chip * 2 + (1 - self.core)
+
+    def across(self, q, k):
+        target = lax.rem(self.chip + k, self.chips) * 2 + self.core
+        return to_sharer(
+            self.source.at[q], self.landing.at[self.me, q],
+            self.out_sems.at[q, k], self.in_sems.at[q, k], target,
+        )
+
+    def over(self, q, k):
+        owner = lax.rem(self.chip + self.chips - k, self.chips) * 2 + self.core
+        piece = self.landing.at[owner, q]
+        return to_sharer(
+            piece, piece, self.pair_out.at[q, k], self.pair_in.at[q, k], self.sibling
+        )
+
+    def own_over(self, q):
+        return to_sharer(
+            self.source.at[q], self.landing.at[self.me, q],
+            self.pair_out.at[q, 0], self.pair_in.at[q, 0], self.sibling,
+        )
+
+    def own(self, q):
+        return pltpu.make_async_copy(
+            self.source.at[q], self.landing.at[self.me, q], self.own_sem.at[q]
+        )
+
+    def each(self, act):
+        def one(k, unused):
+            act(k)
+            return unused
+
+        lax.fori_loop(1, self.chips, one, 0)
+
+    def start(self, q):
+        self.each(lambda k: self.across(q, k).start())
+        self.own_over(q).start()
+        self.own(q).start()
+
+    def forward(self, q):
+        def act(k):
+            self.across(q, k).wait_recv()
+            self.over(q, k).start()
+
+        self.each(act)
+
+    def finish(self, q):
+        def act(k):
+            self.across(q, k).wait_send()
+            self.over(q, k).wait()
+
+        self.each(act)
+        self.own_over(q).wait()
+        self.own(q).wait()
+
+
+def exchange_sems(pieces, chips):
+    return [pltpu.SemaphoreType.DMA((pieces, chips))] * 4 + [pltpu.SemaphoreType.DMA((pieces,))]
+
+
 def forward_kernel(
     order, keep, last_of, filled, acts, gain, tiles,
     out_ref, x_ref, pre_ref, hid_ref,
@@ -123,6 +215,10 @@
 
 def in_smem(count):
     return [pl.BlockSpec(memory_space=pltpu.SMEM)] * count
+
+
+def anywhere(count):
+    return [pl.BlockSpec(memory_space=pl.ANY)] * count
 
 
 def run_forward(tables, acts, gain, gathered):
@@ -160,14 +256,39 @@
 
 
 def backward_kernel(
-    split, cols, lens, cot, gain, tiles, x_in, pre_in,
-    grad_ref, pd_ref,
-    landing, g_all, gained_ref, dot_ref, send_sems, recv_sems,
+    split, tile_count, cols, lens, cot, gain, tiles, x_in, pre_in, hid_in,
+    grad_ref, deltas_ref, hidden_ref,
+    pd_ref, landing, g_all, gained_ref, dot_ref, send_sems, recv_sems,
+    hid_out, hid_arrive, hid_own, *sems
 ):
     chunks, blocks, rows, tile = pre_in.shape
     here, count = lax.axis_index("pipe"), lax.axis_size("pipe")
     target = lax.rem(here + count - 1, count)
-    greet()
+    me, sharers = lax.axis_index("dp"), lax.axis_size("dp")
+    own_rows = hidden_ref.shape[2]
+    deltas = Exchange(pd_ref, deltas_ref, *sems)
+    greet(sharers)
+
+    def rows_of(device):
+        return hid_in.at[:, pl.ds(device * tile_count // KEEP, own_rows)]
+
+    def hidden_to(j):
+        other = lax.rem(me + j, sharers)
+        return to_sharer(
+            rows_of(other), hidden_ref.at[me], hid_out.at[j], hid_arrive.at[j], other
+        )
+
+    def send_hidden(j, unused):
+        hidden_to(j).start()
+        return unused
+
+    def settle_hidden(j, unused):
+        hidden_to(j).wait()
+        return unused
+
+    lax.fori_loop(1, sharers, send_hidden, 0)
+    hidden_here = pltpu.make_async_copy(rows_of(me), hidden_ref.at[me], hid_own)
+    hidden_here.start()
 
     def one_chunk(q, carried):
         copy = hop(grad_ref, landing, send_sems, recv_sems, q, target)
@@ -194,6 +315,7 @@
             pd_ref[q, r] = (g * s * (1.0 + p * (1.0 - s))).astype(BF16)
             v = x_in[q, :, columns(r, tile)].astype(F32)
             total = total + v * v
+        deltas.start(q)
         mean = jnp.sum(total, axis=1, keepdims=True) * (1.0 / (blocks * tile))
         inv = jnp.broadcast_to(lax.rsqrt(mean + EPSILON), (rows, tile))
         dot_ref[...] = jnp.zeros_like(dot_ref)
@@ -234,27 +356,41 @@
         for q in range(chunks):
             hop(grad_ref, landing, send_sems, recv_sems, q, target).wait_send()
 
-
-def run_backward(split, cols, lens, cot, gain, gathered, x_all, pre_all):
+    for act in (deltas.forward, deltas.finish):
+        for q in range(chunks):
+            act(q)
+    lax.fori_loop(1, sharers, settle_hidden, 0)
+    hidden_here.wait()
+
+
+def run_backward(split, tile_count, cols, lens, cot, gain, gathered, x_all, pre_all, hid_all):
     chunks, rows, width = cot.shape
+    sharers = lax.axis_size("dp")
+    own_rows = max(1, tile_count // KEEP)
     tile = gathered.shape[1]
     cut = (width // tile, rows, tile)
     return pl.pallas_call(
-        functools.partial(backward_kernel, split),
-        in_specs=in_smem(2) + in_vmem(5),
-        out_specs=in_vmem(2),
+        functools.partial(backward_kernel, split, tile_count),
+        in_specs=in_smem(2) + in_vmem(5) + anywhere(1),
+        out_specs=in_vmem(1) + anywhere(2),
         out_shape=[
             jax.ShapeDtypeStruct(cot.shape, BF16),
-            jax.ShapeDtypeStruct((chunks, *cut), BF16),
+            jax.ShapeDtypeStruct((sharers, chunks, *cut), BF16),
+            jax.ShapeDtypeStruct((sharers, chunks, own_rows, rows, tile), BF16),
         ],
         scratch_shapes=[
+            pltpu.VMEM((chunks, *cut), BF16),
             pltpu.VMEM(cot.shape, BF16),
             pltpu.VMEM(cut, BF16),
             pltpu.VMEM(cut, F32),
             pltpu.VMEM((rows, tile), F32),
             pltpu.SemaphoreType.DMA((chunks,)),
             pltpu.SemaphoreType.DMA((chunks,)),
-        ],
+            pltpu.SemaphoreType.DMA((sharers,)),
+            pltpu.SemaphoreType.DMA((sharers,)),
+            pltpu.SemaphoreType.DMA,
+        ]
+        + exchange_sems(chunks, sharers // 2),
         compiler_params=pltpu.CompilerParams(
             vmem_limit_bytes=VMEM_BYTES, collective_id=1, has_side_effects=True
         ),
@@ -264,7 +400,7 @@
             transcendentals=chunks * rows * width,
         ),
         name="backward_relay",
-    )(cols, lens, cot, gain, gathered, x_all, pre_all)
+    )(cols, lens, cot, gain, gathered, x_all, pre_all, hid_all)
 
 
 def tile_grad_kernel(per_group, base, cols, hidden, deltas, out_ref):
@@ -297,7 +433,7 @@
 
 
 def run_tile_grad(base, cols, hidden, deltas, tile_count):
-    devices, micros, blocks, rows, tile = hidden.shape
+    devices, micros, blocks, rows, tile = deltas.shape
     per_group = min(tile_count, KEEP)
     share = min(devices, 8)
     return pl.pallas_call(
@@ -308,7 +444,9 @@
             in_specs=[
                 pl.BlockSpec(
                     (share, micros, 1, rows, tile),
-                    lambda i, k, base, cols: (k, 0, (base[0] + i * per_group) // KEEP, 0, 0),
+                    lambda i, k, base, cols: (
+                        k, 0, (base[0] + i * per_group) // KEEP - base[0] // KEEP, 0, 0
+                    ),
                 )
             ]
             + [
@@ -359,12 +497,10 @@
     section_out, x_all, pre_all, hid_all = run_forward(
         tables, acts_in.reshape(chunks), norm_gains, gathered
     )
-    hidden = lax.all_gather(hid_all, "dp", axis=0)
-    input_grad, pd_all = run_backward(
-        SPLIT, cols, lengths[:, 0], cotangent.reshape(chunks), norm_gains, gathered, x_all, pre_all
+    input_grad, deltas, hidden = run_backward(
+        SPLIT, tile_count, cols, lengths[:, 0], cotangent.reshape(chunks), norm_gains, gathered,
+        x_all, pre_all, hid_all,
     )
-    hidden, pd_all = lax.optimization_barrier((hidden, pd_all))
-    deltas = lax.all_gather(pd_all, "dp", axis=0)
     base = (lax.axis_index("dp") * tile_count).astype(jnp.int32).reshape(1)
     weight_grad = run_tile_grad(base, cols, hidden, deltas, tile_count)
     whole = acts_in.shape

time: 255 us -> 232 us (0.910)
  waiting for transfers between devices: 109 us -> 57 us
  Pallas kernels: 123 us -> 153 us
  local copies, waits for them, and re-layouts: 6.8 us -> 3.89 us
    all_gather x2 -> x0, waiting for transfers between devices: 51.8 us -> none  [the longest x1 51.8 us: on_device(): deltas = lax.all_gather(pd_all, 'dp', axis=0)]
    pallas_call x1, Pallas kernels: 80.7 us -> 112 us  [run_backward(): pl.pallas_call(functools.partial(backward_kernel, split, tile_count), in_...]
    unnamed x22 -> x12, local copies, waits for them, and re-layouts: 6.8 us -> 3.89 us
  transfers between devices with their start and end apart: 3 -> 1, of which waited for: 2 -> 1; matrix products, arithmetic and copies ran while one was open for 1% -> 1% of each run, Pallas kernels for 32% -> 0%
where the time goes in v2:
time: 232 us; the launch traced here: 231 us
  Pallas kernels  153 us (66%)
  waiting for transfers between devices  57 us (25%)
  between operations  14.1 us (6%)
  local copies, waits for them, and re-layouts  3.89 us (2%)
  other arithmetic  2.74 us (1%)
    pallas_call x1, Pallas kernels, run_backward(): pl.pallas_call(functools.partial(backward_kernel, split, tile_count), in_...  112 us
    all_gather x1, waiting for transfers between devices, on_device(): gathered = lax.all_gather(weights[0], 'dp', axis=0, tiled=True)  56.4 us
    pallas_call x1, Pallas kernels, run_forward(): pl.pallas_call(forward_kernel, in_specs=in_smem(4) + in_vmem(3), out_spec...  34.3 us
    pallas_call x1, Pallas kernels, run_tile_grad(): pl.pallas_call(functools.partial(tile_grad_kernel, per_group), grid_spec=...  7.12 us
  transfers between devices with their start and end apart: 1, of which 1 were waited for; matrix products, arithmetic and copies ran while one was open for 1% of the time, Pallas kernels for 0%

profile of v2, /device:TPU:0, one launch (start us, length us, event | category | flops | bytes accessed | tf_op | source)
XLA Modules:
  0.0 231.3 jit_solution(13257034494691821507)
XLA Ops:
  7.2 0.0 copy-start.3
  7.2 0.0 copy-start.4
  7.2 0.0 copy-start.1
  7.2 0.0 all-gather.3.cloned.1.call-start
  7.2 0.7 all-gather.3.cloned.1.call-update
  7.9 0.9 convert_reduce_fusion
  8.9 0.8 select_reduce_fusion
  9.7 0.1 slice_compare_fusion
  9.8 0.1 add_convert_fusion.keep
  9.9 0.8 convert_reduce_fusion.1
  10.7 56.4 %all-gather.3.cloned.1.call-done = bf16[1,256,128,128]{3,2,0,1:T(8,128)(2,1)} async-done(((bf16[1,32,128,128]{3,2,0,1:T(8,128)(2,1)}), bf16[1,256,128,128]{3,2,0,1:T(8,128)(2,1)}) %all-gather.3.cloned.1.call-update) | async-done | bytes 8388624 | tf_op jit(solution)/shard_map/all_gather | solution.py:495
  67.0 0.0 copy-start
  67.0 1.2 copy-done
  68.3 0.0 copy-start.2
  68.3 0.7 copy-done.2
  69.0 34.3 %forward_relay.1 = (bf16[4,32,4096]{2,1,0:T(8,128)(2,1)S(1)}, bf16[4,32,4096]{2,1,0:T(8,128)(2,1)S(1)}, f32[4,32,32,128]{3,2,1,0:T(8,128)}, bf16[4,32,32,128]{3,2,1,0:T(8,128)(2,1)S(1)}) custom-call(s32[256]{0:T(256)S(1)} %get-tuple-element.20.order, f32[256]{0:T(256)S(1)} %add_convert_fusion.keep, s32[32]{0:T(128)S(1)} %add_maximum_fusion.last_of, ...), custom_call_target="tpu_custom_call" | custom-call | flops 1073741824 | bytes 8388608 | tf_op jit(solution)/shard_map/forward_relay/pallas_call | solution.py:229
  103.3 0.0 copy-done.3
  103.3 0.0 copy-done.4
  103.3 0.0 copy-done.1
  103.3 112.0 %backward_relay.1 = (bf16[4,32,4096]{2,1,0:T(8,128)(2,1)S(1)}, bf16[8,4,32,32,128]{4,3,2,1,0:T(8,128)(2,1)}, bf16[8,4,4,32,128]{4,3,2,1,0:T(8,128)(2,1)S(1)}) custom-call(s32[256]{0:T(256)S(1)} %bitcast.17, s32[2]{0:T(128)S(1)} %bitcast.19, bf16[4,32,4096]{2,1,0:T(8,128)(2,1)S(1)} %bitcast.13, f32[1,4096]{1,0:T(1,128)S(1)} %copy-done.2, ...), custom_call_target="tpu_custom_call" | custom-call | flops 1073741824 | bytes 8388608 | tf_op jit(solution)/shard_map/backward_relay/pallas_call | solution.py:372
  215.4 7.1 %tile_grad.1 = f32[32,128,128]{2,1,0:T(8,128)} custom-call(s32[1]{0:T(128)} %bitcast.8.base, s32[256]{0:T(256)S(1)} %bitcast.18, bf16[8,4,4,32,128]{4,3,2,1,0:T(8,128)(2,1)S(1)} %get-tuple-element.15.hidden, bf16[8,4,32,32,128]{4,3,2,1,0:T(8,128)(2,1)} %get-tuple-element.16.deltas), custom_call_target="tpu_custom_call" | custom-call | flops 1073741824 | bytes 8388608 | tf_op jit(solution)/shard_map/tile_grad/pallas_call | solution.py:439
  222.5 1.0 copy.13
  223.5 1.0 copy.14
  (2 shorter events, 0.0 us)
Async XLA Ops:
  7.2 96.2 %copy-start.3 = (s32[1,256]{1,0:T(1,128)S(1)}, s32[1,256]{1,0:T(1,128)}, u32[]{:S(2)}) copy-start(s32[1,256]{1,0:T(1,128)} %param.10) | copy-start | bytes 3076
  7.2 96.2 %copy-start.4 = (s32[2,1]{0,1:T(1,128)S(1)}, s32[2,1]{0,1:T(1,128)}, u32[]{:S(2)}) copy-start(s32[2,1]{0,1:T(1,128)} %param.11) | copy-start | bytes 28
  7.2 96.2 %copy-start.1 = (bf16[2,64,4096]{2,1,0:T(8,128)(2,1)S(1)}, bf16[2,64,4096]{2,1,0:T(8,128)(2,1)}, u32[]{:S(2)}) copy-start(bf16[2,64,4096]{2,1,0:T(8,128)(2,1)} %param.7) | copy-start | bytes 3145732
  7.2 59.8 %all-gather.3.cloned.1.call-start = ((), (), s32[]{:S(2)}) async-start(), calls=%async_computation | async-start | bytes 9437184 | tf_op jit(solution)/shard_map/all_gather | solution.py:495
  67.0 1.2 copy-start
  68.3 0.7 copy-start.2
Sparse Core Ops, SparseCore 0:
  9.9 57.0 all-gather.2

commit v3 on v2

--- a/solution.py
+++ b/solution.py
@@ -11,6 +11,7 @@
 EPSILON = 1e-05
 ROWS_PER_STEP = 4
 SPLIT = 2
+PIECES = 4
 VMEM_BYTES = 48 * 1024 * 1024
 
 F32 = jnp.float32
@@ -79,17 +80,63 @@
         self.chips = lax.axis_size("dp") // 2
         self.chip, self.core = self.me // 2, lax.rem(self.me, 2)
         self.sibling = self.chip * 2 + (1 - self.core)
+        self.square = self.chips == 4
+        if self.square:
+            low, high = lax.rem(self.chip, 2), self.chip // 2
+            self.near = {
+                1: (high * 2 + 1 - low) * 2 + self.core,
+                2: ((1 - high) * 2 + low) * 2 + self.core,
+                3: ((1 - high) * 2 + 1 - low) * 2 + self.core,
+            }
+
+    def half(self, owner, q, which):
+        size = self.landing.shape[2] // 2
+        return self.landing.at[owner, q, pl.ds(which * size, size)]
 
     def across(self, q, k):
-        target = lax.rem(self.chip + k, self.chips) * 2 + self.core
+        if self.square:
+            target = self.near[k]
+        else:
+            target = lax.rem(self.chip + k, self.chips) * 2 + self.core
         return to_sharer(
             self.source.at[q], self.landing.at[self.me, q],
             self.out_sems.at[q, k], self.in_sems.at[q, k], target,
         )
 
+    def passed_on(self, q, k):
+        piece = self.half(self.near[k], q, k - 1)
+        return to_sharer(
+            piece, piece, self.out_sems.at[q, 2 + k], self.in_sems.at[q, 2 + k], self.near[3 - k]
+        )
+
+    def passed_here(self, q, k):
+        piece = self.half(self.near[3], q, k - 1)
+        return to_sharer(
+            piece, piece, self.out_sems.at[q, 2 + k], self.in_sems.at[q, 2 + k], self.near[3 - k]
+        )
+
     def over(self, q, k):
-        owner = lax.rem(self.chip + self.chips - k, self.chips) * 2 + self.core
-        piece = self.landing.at[owner, q]
+        if self.square and k > 2:
+            piece = self.half(self.near[3], q, k - 3)
+        elif self.square:
+            piece = self.landing.at[self.near[k], q]
+        else:
+            owner = lax.rem(self.chip + self.chips - k, self.chips) * 2 + self.core
+            piece = self.landing.at[owner, q]
+        return to_sharer(
+            piece, piece, self.pair_out.at[q, k], self.pair_in.at[q, k], self.sibling
+        )
+
+    def over_here(self, q, k):
+        if self.square:
+            flip = 1 - 2 * self.core
+            if k > 2:
+                piece = self.half(self.near[3] + flip, q, k - 3)
+            else:
+                piece = self.landing.at[self.near[k] + flip, q]
+        else:
+            owner = lax.rem(self.chip + self.chips - k, self.chips) * 2 + 1 - self.core
+            piece = self.landing.at[owner, q]
         return to_sharer(
             piece, piece, self.pair_out.at[q, k], self.pair_in.at[q, k], self.sibling
         )
@@ -110,7 +157,11 @@
             act(k)
             return unused
 
-        lax.fori_loop(1, self.chips, one, 0)
+        if self.square:
+            act(1)
+            act(2)
+        else:
+            lax.fori_loop(1, self.chips, one, 0)
 
     def start(self, q):
         self.each(lambda k: self.across(q, k).start())
@@ -120,33 +171,59 @@
     def forward(self, q):
         def act(k):
             self.across(q, k).wait_recv()
+            if self.square:
+                self.passed_on(q, k).start()
             self.over(q, k).start()
 
         self.each(act)
 
-    def finish(self, q):
+    def last_forward(self, q):
+        if self.square:
+            for k in (1, 2):
+                self.passed_here(q, k).wait_recv()
+                self.over(q, 2 + k).start()
+
+    def arrive(self, q):
+        self.each(lambda k: self.over_here(q, k).wait_recv())
+        if self.square:
+            for k in (3, 4):
+                self.over_here(q, k).wait_recv()
+        self.own_over(q).wait_recv()
+        self.own(q).wait()
+
+    def sent(self, q):
         def act(k):
             self.across(q, k).wait_send()
-            self.over(q, k).wait()
+            self.over(q, k).wait_send()
 
         self.each(act)
-        self.own_over(q).wait()
-        self.own(q).wait()
+        if self.square:
+            for k in (1, 2):
+                self.passed_on(q, k).wait_send()
+                self.over(q, 2 + k).wait_send()
+        self.own_over(q).wait_send()
 
 
 def exchange_sems(pieces, chips):
-    return [pltpu.SemaphoreType.DMA((pieces, chips))] * 4 + [pltpu.SemaphoreType.DMA((pieces,))]
+    width = max(chips, 5)
+    return [pltpu.SemaphoreType.DMA((pieces, width))] * 4 + [pltpu.SemaphoreType.DMA((pieces,))]
 
 
 def forward_kernel(
-    order, keep, last_of, filled, acts, gain, tiles,
-    out_ref, x_ref, pre_ref, hid_ref,
-    landing, parts_ref, sums_ref, send_sems, recv_sems,
+    order, keep, last_of, filled, acts, gain, share,
+    out_ref, x_ref, pre_ref, hid_ref, all_tiles,
+    landing, parts_ref, sums_ref, send_sems, recv_sems, *sems
 ):
     chunks, blocks, rows, tile = pre_ref.shape
     here, count = lax.axis_index("pipe"), lax.axis_size("pipe")
     target = lax.rem(here + 1, count)
-    greet()
+    pieces = share.shape[0]
+    weights = Exchange(share, all_tiles, *sems)
+    tiles = all_tiles.reshape(parts_ref.shape[0], tile, tile)
+    greet(lax.axis_size("dp"))
+    for act in (weights.start, weights.forward, weights.last_forward, weights.arrive):
+        for q in range(pieces):
+            act(q)
 
     def one_chunk(q, carried):
         copy = hop(out_ref, landing, send_sems, recv_sems, q, target)
@@ -208,6 +285,9 @@
         for q in range(chunks):
             hop(out_ref, landing, send_sems, recv_sems, q, target).wait_send()
 
+    for q in range(pieces):
+        weights.sent(q)
+
 
 def in_vmem(count):
     return [pl.BlockSpec(memory_space=pltpu.VMEM)] * count
@@ -221,20 +301,23 @@
     return [pl.BlockSpec(memory_space=pl.ANY)] * count
 
 
-def run_forward(tables, acts, gain, gathered):
+def run_forward(tables, acts, gain, share):
     chunks, rows, width = acts.shape
-    tile_total, tile, _ = gathered.shape
+    pieces, tile = share.shape[0], share.shape[2]
+    sharers = lax.axis_size("dp")
     blocks = width // tile
+    tile_total = blocks * KEEP
     cut = (blocks, rows, tile)
     return pl.pallas_call(
         forward_kernel,
         in_specs=in_smem(4) + in_vmem(3),
-        out_specs=in_vmem(4),
+        out_specs=in_vmem(5),
         out_shape=[
             jax.ShapeDtypeStruct(acts.shape, BF16),
             jax.ShapeDtypeStruct(acts.shape, BF16),
             jax.ShapeDtypeStruct((chunks, *cut), F32),
             jax.ShapeDtypeStruct((chunks, *cut), BF16),
+            jax.ShapeDtypeStruct((sharers, *share.shape), BF16),
         ],
         scratch_shapes=[
             pltpu.VMEM(acts.shape, BF16),
@@ -242,17 +325,18 @@
             pltpu.VMEM((tile_total, rows, tile), F32),
             pltpu.SemaphoreType.DMA((chunks,)),
             pltpu.SemaphoreType.DMA((chunks,)),
-        ],
+        ]
+        + exchange_sems(pieces, sharers // 2),
         compiler_params=pltpu.CompilerParams(
             vmem_limit_bytes=VMEM_BYTES, collective_id=0, has_side_effects=True
         ),
         cost_estimate=pl.CostEstimate(
             flops=2 * chunks * rows * KEEP * width * tile,
-            bytes_accessed=gathered.size * 2,
+            bytes_accessed=sharers * share.size * 2,
             transcendentals=chunks * rows * width,
         ),
         name="forward_relay",
-    )(*tables, acts, gain, gathered)
+    )(*tables, acts, gain, share)
 
 
 def backward_kernel(
@@ -347,18 +431,29 @@
         def _():
             copy.start()
 
+        @pl.when(jnp.logical_and(here == 0, q > 0))
+        def _():
+            deltas.forward(q - 1)
+
         return carried
 
     lax.fori_loop(0, chunks, one_chunk, 0)
+
+    @pl.when(here > 0)
+    def _():
+        for q in range(chunks - 1):
+            deltas.forward(q)
+
+    deltas.forward(chunks - 1)
+    for act in (deltas.last_forward, deltas.arrive, deltas.sent):
+        for q in range(chunks):
+            act(q)
 
     @pl.when(here > 0)
     def _():
         for q in range(chunks):
             hop(grad_ref, landing, send_sems, recv_sems, q, target).wait_send()
 
-    for act in (deltas.forward, deltas.finish):
-        for q in range(chunks):
-            act(q)
     lax.fori_loop(1, sharers, settle_hidden, 0)
     hidden_here.wait()
 
@@ -492,11 +587,12 @@
     cols = tile_columns[0]
     tile_count, tile = weights.shape[1:3]
     chunks = (micros * SPLIT, rows // SPLIT, width)
-    gathered = lax.all_gather(weights[0], "dp", axis=0, tiled=True)
+    share = weights[0].reshape(PIECES, tile_count // PIECES, tile, tile)
     tables = column_order(cols, width // tile)
-    section_out, x_all, pre_all, hid_all = run_forward(
-        tables, acts_in.reshape(chunks), norm_gains, gathered
+    section_out, x_all, pre_all, hid_all, gathered = run_forward(
+        tables, acts_in.reshape(chunks), norm_gains, share
     )
+    gathered = gathered.reshape(-1, tile, tile)
     input_grad, deltas, hidden = run_backward(
         SPLIT, tile_count, cols, lengths[:, 0], cotangent.reshape(chunks), norm_gains, gathered,
         x_all, pre_all, hid_all,

time: 232 us -> 194 us (0.84)
  waiting for transfers between devices: 57 us -> 0 us
  Pallas kernels: 153 us -> 183 us
  between operations: 14.1 us -> 0.69 us
  local copies, waits for them, and re-layouts: 3.89 us -> 7.66 us
    all_gather x1 -> x0, waiting for transfers between devices: 56.4 us -> none  [on_device(): gathered = lax.all_gather(weights[0], 'dp', axis=0, tiled=True)]
    pallas_call x1, Pallas kernels: 34.3 us -> 72.3 us  [run_forward(): pl.pallas_call(forward_kernel, in_specs=in_smem(4) + in_vmem(3), out_spec...]
    pallas_call x1, Pallas kernels: 112 us -> 103 us  [run_backward(): pl.pallas_call(functools.partial(backward_kernel, split, tile_count), in_...]
    unnamed x12 -> x16, local copies, waits for them, and re-layouts: 3.89 us -> 7.66 us
  transfers between devices with their start and end apart: 1 -> 0, of which waited for: 1 -> 0; matrix products, arithmetic and copies ran while one was open for 1% -> 0% of each run, Pallas kernels for 0% -> 0%
where the time goes in v3:
time: 194 us
  Pallas kernels  183 us (94%)
  local copies, waits for them, and re-layouts  7.66 us (4%)
  other arithmetic  2.74 us (1%)
    pallas_call x1, Pallas kernels, run_backward(): pl.pallas_call(functools.partial(backward_kernel, split, tile_count), in_...  103 us
    pallas_call x1, Pallas kernels, run_forward(): pl.pallas_call(forward_kernel, in_specs=in_smem(4) + in_vmem(3), out_spec...  72.3 us
    unnamed x16, local copies, waits for them, and re-layouts  7.66 us
    pallas_call x1, Pallas kernels, run_tile_grad(): pl.pallas_call(functools.partial(tile_grad_kernel, per_group), grid_spec=...  7.12 us

profile of v3, /device:TPU:0, one launch (start us, length us, event | category | flops | bytes accessed | tf_op | source)
XLA Modules:
  0.0 193.9 jit_solution(10205171333473389507)
XLA Ops:
  0.6 0.9 convert_reduce_fusion
  1.6 0.8 select_reduce_fusion
  2.4 0.1 slice_compare_fusion
  2.5 0.1 add_convert_fusion.keep
  2.6 0.8 convert_reduce_fusion.1
  3.4 0.0 copy-start.3
  3.4 0.7 copy-done.3
  4.1 0.0 copy-start.5
  4.1 1.2 copy-done.5
  5.3 0.0 copy-start.6
  5.3 1.2 copy-done.6
  6.6 0.0 copy-start.2
  6.6 72.3 %forward_relay.1 = (bf16[4,32,4096]{2,1,0:T(8,128)(2,1)S(1)}, bf16[4,32,4096]{2,1,0:T(8,128)(2,1)S(1)}, f32[4,32,32,128]{3,2,1,0:T(8,128)}, bf16[4,32,32,128]{3,...) custom-call(s32[256]{0:T(256)S(1)} %get-tuple-element.22.order, f32[256]{0:T(256)S(1)} %add_convert_fusion.keep, ...), custom_call_target="tpu_custom_call" | custom-call | flops 1073741824 | bytes 8388608 | tf_op jit(solution)/shard_map/forward_relay/pallas_call | solution.py:311
  78.8 0.0 copy-start
  78.8 1.2 copy-done
  80.0 0.0 copy-start.1
  80.0 0.7 copy-done.1
  80.7 0.0 copy-start.4
  80.7 0.7 copy-done.4
  81.4 103.4 %backward_relay.1 = (bf16[4,32,4096]{2,1,0:T(8,128)(2,1)S(1)}, bf16[8,4,32,32,128]{4,3,2,1,0:T(8,128)(2,1)}, bf16[8,4,4,32,128]{4,3,2,1,0:T(8,128)(2,1)S(1)}) custom-call(s32[256]{0:T(256)S(1)} %bitcast.16, s32[2]{0:T(128)S(1)} %bitcast.18, bf16[4,32,4096]{2,1,0:T(8,128)(2,1)S(1)} %bitcast.12, f32[1,4096]{1,0:T(1,128)S(1)} %copy-done.3, ...), custom_call_target="tpu_custom_call" | custom-call | flops 1073741824 | bytes 8388608 | tf_op jit(solution)/shard_map/backward_relay/pallas_call | solution.py:467
  184.8 0.0 copy-done.2
  184.8 7.1 %tile_grad.1 = f32[32,128,128]{2,1,0:T(8,128)} custom-call(s32[1]{0:T(128)} %bitcast.8.base, s32[256]{0:T(256)S(1)} %bitcast.17, bf16[8,4,4,32,128]{4,3,2,1,0:T(8,128)(2,1)S(1)} %get-tuple-element.17.hidden, bf16[8,4,32,32,128]{4,3,2,1,0:T(8,128)(2,1)} %get-tuple-element.18.deltas), custom_call_target="tpu_custom_call" | custom-call | flops 1073741824 | bytes 8388608 | tf_op jit(solution)/shard_map/tile_grad/pallas_call | solution.py:534
  191.9 1.0 copy.11
  192.9 1.0 copy.12
  (2 shorter events, 0.0 us)
Async XLA Ops:
  3.4 0.7 copy-start.3
  4.1 1.2 copy-start.5
  5.3 1.2 copy-start.6
  6.6 178.3 %copy-start.2 = (s32[1,256]{1,0:T(1,128)S(1)}, s32[1,256]{1,0:T(1,128)}, u32[]{:S(2)}) copy-start(s32[1,256]{1,0:T(1,128)} %param.10) | copy-start | bytes 3076
  78.8 1.2 copy-start
  80.0 0.7 copy-start.1
  80.7 0.7 copy-start.4

commit v4 on v3

--- a/solution.py
+++ b/solution.py
@@ -11,7 +11,7 @@
 EPSILON = 1e-05
 ROWS_PER_STEP = 4
 SPLIT = 2
-PIECES = 4
+PIECES = 8
 VMEM_BYTES = 48 * 1024 * 1024
 
 F32 = jnp.float32
@@ -212,7 +212,7 @@
 def forward_kernel(
     order, keep, last_of, filled, acts, gain, share,
     out_ref, x_ref, pre_ref, hid_ref, all_tiles,
-    landing, parts_ref, sums_ref, send_sems, recv_sems, *sems
+    landing, parts_ref, sums_ref, send_sems, recv_sems, first_sem, *sems
 ):
     chunks, blocks, rows, tile = pre_ref.shape
     here, count = lax.axis_index("pipe"), lax.axis_size("pipe")
@@ -221,22 +221,28 @@
     weights = Exchange(share, all_tiles, *sems)
     tiles = all_tiles.reshape(parts_ref.shape[0], tile, tile)
     greet(lax.axis_size("dp"))
+    first = pltpu.make_async_copy(acts, landing, first_sem)
+
+    @pl.when(here == 0)
+    def _():
+        first.start()
+
     for act in (weights.start, weights.forward, weights.last_forward, weights.arrive):
         for q in range(pieces):
             act(q)
 
+    @pl.when(here == 0)
+    def _():
+        first.wait()
+
     def one_chunk(q, carried):
         copy = hop(out_ref, landing, send_sems, recv_sems, q, target)
-
-        @pl.when(here == 0)
-        def _():
-            x_ref[q] = acts[q]
 
         @pl.when(here > 0)
         def _():
             copy.wait_recv()
-            x_ref[q] = landing[q]
-
+
+        x_ref[q] = landing[q]
         total = jnp.zeros((rows, tile), F32)
         for r in range(blocks):
             v = x_ref[q, :, columns(r, tile)].astype(F32)
@@ -310,7 +316,7 @@
     cut = (blocks, rows, tile)
     return pl.pallas_call(
         forward_kernel,
-        in_specs=in_smem(4) + in_vmem(3),
+        in_specs=in_smem(4) + anywhere(1) + in_vmem(1) + anywhere(1),
         out_specs=in_vmem(5),
         out_shape=[
             jax.ShapeDtypeStruct(acts.shape, BF16),
@@ -325,6 +331,7 @@
             pltpu.VMEM((tile_total, rows, tile), F32),
             pltpu.SemaphoreType.DMA((chunks,)),
             pltpu.SemaphoreType.DMA((chunks,)),
+            pltpu.SemaphoreType.DMA,
         ]
         + exchange_sems(pieces, sharers // 2),
         compiler_params=pltpu.CompilerParams(
@@ -343,7 +350,7 @@
     split, tile_count, cols, lens, cot, gain, tiles, x_in, pre_in, hid_in,
     grad_ref, deltas_ref, hidden_ref,
     pd_ref, landing, g_all, gained_ref, dot_ref, send_sems, recv_sems,
-    hid_out, hid_arrive, hid_own, *sems
+    hid_out, hid_arrive, hid_own, first_sem, *sems
 ):
     chunks, blocks, rows, tile = pre_in.shape
     here, count = lax.axis_index("pipe"), lax.axis_size("pipe")
@@ -351,6 +358,12 @@
     me, sharers = lax.axis_index("dp"), lax.axis_size("dp")
     own_rows = hidden_ref.shape[2]
     deltas = Exchange(pd_ref, deltas_ref, *sems)
+    first = pltpu.make_async_copy(cot, landing, first_sem)
+
+    @pl.when(here == count - 1)
+    def _():
+        first.start()
+
     greet(sharers)
 
     def rows_of(device):
@@ -373,6 +386,11 @@
     lax.fori_loop(1, sharers, send_hidden, 0)
     hidden_here = pltpu.make_async_copy(rows_of(me), hidden_ref.at[me], hid_own)
     hidden_here.start()
+
+    @pl.when(here == count - 1)
+    def _():
+        first.wait()
+
 
     def one_chunk(q, carried):
         copy = hop(grad_ref, landing, send_sems, recv_sems, q, target)
@@ -383,7 +401,7 @@
             place = lax.broadcasted_iota(jnp.int32, (rows, tile), 0) + start
             valid = (place < lens[q // split]).astype(F32)
             for r in range(blocks):
-                g_all[r] = (cot[q, :, columns(r, tile)].astype(F32) * valid).astype(BF16)
+                g_all[r] = (landing[q, :, columns(r, tile)].astype(F32) * valid).astype(BF16)
 
         @pl.when(here < count - 1)
         def _():
@@ -466,7 +484,7 @@
     cut = (width // tile, rows, tile)
     return pl.pallas_call(
         functools.partial(backward_kernel, split, tile_count),
-        in_specs=in_smem(2) + in_vmem(5) + anywhere(1),
+        in_specs=in_smem(2) + anywhere(1) + in_vmem(4) + anywhere(1),
         out_specs=in_vmem(1) + anywhere(2),
         out_shape=[
             jax.ShapeDtypeStruct(cot.shape, BF16),
@@ -484,6 +502,7 @@
             pltpu.SemaphoreType.DMA((sharers,)),
             pltpu.SemaphoreType.DMA((sharers,)),
             pltpu.SemaphoreType.DMA,
+            pltpu.SemaphoreType.DMA,
         ]
         + exchange_sems(chunks, sharers // 2),
         compiler_params=pltpu.CompilerParams(
@@ -500,46 +519,41 @@
 
 def tile_grad_kernel(per_group, base, cols, hidden, deltas, out_ref):
     share, micros, _, rows, tile = hidden.shape
-    start = base[0] + pl.program_id(0) * per_group
-    total = None
-    for m in range(micros):
-        left = hidden[:, m, 0].reshape(share * rows, tile)
-        right = jnp.concatenate(
-            [
-                deltas[:, m, cols[start + j]].reshape(share * rows, tile)
-                for j in range(per_group)
-            ],
-            axis=1,
-        )
-        term = lax.dot_general(
-            left, right, (((0,), (0,)), ((), ())), preferred_element_type=F32
-        )
-        total = term if total is None else total + term
-
-    @pl.when(pl.program_id(1) == 0)
+    group = pl.program_id(1)
+    start = base[0] + group * per_group
+    depth = share * micros * rows
+    right = jnp.concatenate(
+        [deltas[:, :, cols[start + j]].reshape(depth, tile) for j in range(per_group)], axis=1
+    )
+    total = lax.dot_general(
+        hidden[:, :, 0].reshape(depth, tile), right, (((0,), (0,)), ((), ())),
+        preferred_element_type=F32,
+    )
+
+    @pl.when(pl.program_id(0) == 0)
     def _():
         for j in range(per_group):
-            out_ref[j] = total[:, j * tile : (j + 1) * tile]
-
-    @pl.when(pl.program_id(1) > 0)
+            out_ref[group * per_group + j] = total[:, j * tile : (j + 1) * tile]
+
+    @pl.when(pl.program_id(0) > 0)
     def _():
         for j in range(per_group):
-            out_ref[j] += total[:, j * tile : (j + 1) * tile]
+            out_ref[group * per_group + j] += total[:, j * tile : (j + 1) * tile]
 
 
 def run_tile_grad(base, cols, hidden, deltas, tile_count):
     devices, micros, blocks, rows, tile = deltas.shape
     per_group = min(tile_count, KEEP)
-    share = min(devices, 8)
+    share = min(devices, 2)
     return pl.pallas_call(
         functools.partial(tile_grad_kernel, per_group),
         grid_spec=pltpu.PrefetchScalarGridSpec(
             num_scalar_prefetch=2,
-            grid=(tile_count // per_group, devices // share),
+            grid=(devices // share, tile_count // per_group),
             in_specs=[
                 pl.BlockSpec(
                     (share, micros, 1, rows, tile),
-                    lambda i, k, base, cols: (
+                    lambda k, i, base, cols: (
                         k, 0, (base[0] + i * per_group) // KEEP - base[0] // KEEP, 0, 0
                     ),
                 )
@@ -547,11 +561,11 @@
             + [
                 pl.BlockSpec(
                     (share, micros, blocks, rows, tile),
-                    lambda i, k, base, cols: (k, 0, 0, 0, 0),
+                    lambda k, i, base, cols: (k, 0, 0, 0, 0),
                 )
             ],
             out_specs=pl.BlockSpec(
-                (per_group, tile, tile), lambda i, k, base, cols: (i, 0, 0)
+                (tile_count, tile, tile), lambda k, i, base, cols: (0, 0, 0)
             ),
         ),
         out_shape=jax.ShapeDtypeStruct((tile_count, tile, tile), F32),
@@ -587,7 +601,8 @@
     cols = tile_columns[0]
     tile_count, tile = weights.shape[1:3]
     chunks = (micros * SPLIT, rows // SPLIT, width)
-    share = weights[0].reshape(PIECES, tile_count // PIECES, tile, tile)
+    pieces = min(PIECES, tile_count)
+    share = weights[0].reshape(pieces, tile_count // pieces, tile, tile)
     tables = column_order(cols, width // tile)
     section_out, x_all, pre_all, hid_all, gathered = run_forward(
         tables, acts_in.reshape(chunks), norm_gains, share

time: 194 us -> 201 us (1.036)
  Pallas kernels: 183 us -> 190 us
    pallas_call x1, Pallas kernels: 7.12 us -> 12.8 us  [run_tile_grad(): pl.pallas_call(functools.partial(tile_grad_kernel, per_group), grid_spec=...]
where the time goes in v4:
time: 201 us
  Pallas kernels  190 us (95%)
  local copies, waits for them, and re-layouts  7.66 us (4%)
  other arithmetic  2.74 us (1%)
    pallas_call x1, Pallas kernels, run_backward(): pl.pallas_call(functools.partial(backward_kernel, split, tile_count), in_...  103 us
    pallas_call x1, Pallas kernels, run_forward(): pl.pallas_call(forward_kernel, in_specs=in_smem(4) + anywhere(1) + in_vme...  73.4 us
    pallas_call x1, Pallas kernels, run_tile_grad(): pl.pallas_call(functools.partial(tile_grad_kernel, per_group), grid_spec=...  12.8 us
    unnamed x16, local copies, waits for them, and re-layouts  7.66 us

profile of v4, /device:TPU:0, one launch (start us, length us, event | category | flops | bytes accessed | tf_op | source)
XLA Modules:
  0.0 200.7 jit_solution(10216024553225312339)
XLA Ops:
  0.6 0.9 convert_reduce_fusion
  1.6 0.8 select_reduce_fusion
  2.4 0.1 slice_compare_fusion
  2.5 0.1 add_convert_fusion.keep
  2.6 0.8 convert_reduce_fusion.1
  3.4 0.0 copy-start.3
  3.4 0.7 copy-done.3
  4.1 0.0 copy-start.5
  4.1 1.2 copy-done.5
  5.3 0.0 copy-start.6
  5.3 1.2 copy-done.6
  6.6 0.0 copy-start.2
  6.6 73.4 %forward_relay.1 = (bf16[4,32,4096]{2,1,0:T(8,128)(2,1)S(1)}, bf16[4,32,4096]{2,1,0:T(8,128)(2,1)S(1)}, f32[4,32,32,128]{3,2,1,0:T(8,128)}, bf16[4,32,32,128]{3,...) custom-call(s32[256]{0:T(256)S(1)} %get-tuple-element.22.order, f32[256]{0:T(256)S(1)} %add_convert_fusion.keep, ...), custom_call_target="tpu_custom_call" | custom-call | flops 1073741824 | bytes 8388608 | tf_op jit(solution)/shard_map/forward_relay/pallas_call | solution.py:317
  80.0 0.0 copy-start
  80.0 1.2 copy-done
  81.2 0.0 copy-start.1
  81.2 0.7 copy-done.1
  81.9 0.0 copy-start.4
  81.9 0.7 copy-done.4
  82.5 103.4 %backward_relay.1 = (bf16[4,32,4096]{2,1,0:T(8,128)(2,1)S(1)}, bf16[8,4,32,32,128]{4,3,2,1,0:T(8,128)(2,1)}, bf16[8,4,4,32,128]{4,3,2,1,0:T(8,128)(2,1)S(1)}) custom-call(s32[256]{0:T(256)S(1)} %bitcast.16, s32[2]{0:T(128)S(1)} %bitcast.18, bf16[4,32,4096]{2,1,0:T(8,128)(2,1)S(1)} %bitcast.12, f32[1,4096]{1,0:T(1,128)S(1)} %copy-done.3, ...), custom_call_target="tpu_custom_call" | custom-call | flops 1073741824 | bytes 8388608 | tf_op jit(solution)/shard_map/backward_relay/pallas_call | solution.py:485
  186.0 0.0 copy-done.2
  186.0 12.8 %tile_grad.1 = f32[32,128,128]{2,1,0:T(8,128)} custom-call(s32[1]{0:T(128)} %bitcast.8.base, s32[256]{0:T(256)S(1)} %bitcast.17, bf16[8,4,4,32,128]{4,3,2,1,0:T(8,128)(2,1)S(1)} %get-tuple-element.17.hidden, bf16[8,4,32,32,128]{4,3,2,1,0:T(8,128)(2,1)} %get-tuple-element.18.deltas), custom_call_target="tpu_custom_call" | custom-call | flops 1073741824 | bytes 8388608 | tf_op jit(solution)/shard_map/tile_grad/pallas_call | solution.py:548
  198.8 1.0 copy.11
  199.8 1.0 copy.12
  (2 shorter events, 0.0 us)
Async XLA Ops:
  3.4 0.7 copy-start.3
  4.1 1.2 copy-start.5
  5.3 1.2 copy-start.6
  6.6 179.4 %copy-start.2 = (s32[1,256]{1,0:T(1,128)S(1)}, s32[1,256]{1,0:T(1,128)}, u32[]{:S(2)}) copy-start(s32[1,256]{1,0:T(1,128)} %param.10) | copy-start | bytes 3076
  80.0 1.2 copy-start
  81.2 0.7 copy-start.1
  81.9 0.7 copy-start.4
